TPU v7x, 128 devices: a whole 4x4x4 slice. The times are simulated.
128 devices in a mesh: loop: 16 (over x_lo, z, core), slab: 8 (over y, x_hi).
Axes of the slice: x: 4 (x_hi: 2, x_lo: 2; x = x_hi * 2 + x_lo), y: 4, z: 4, core: 2. Of those that a mesh axis runs over, the one named last changes fastest.
Arguments:
- signal: bfloat16 [32, 64, 64, 1920], P('slab', 'loop'), may hold values from -6 to 6
- width_class: int32 [32, 64, 64], P('slab', 'loop'), may hold values from 0 to 3
- kernel: float32 [3, 4], replicated, may hold values from 0.04 to 0.16
- taps: float32 [9], replicated, may hold values from 0.05 to 0.4
- chosen: int32 [16, 8, 512], P('loop', 'slab'), may hold values from 0 to 1023, as said below
Outputs:
- tiles: bfloat16 [8192, 8, 8192], P('loop', 'slab')
Inputs may be any that keep to these rules, and one draw needn't show every extreme that they name: `chosen`: within one device the entries are distinct; 0 and 1023 occur on every device.
All inputs are finite; a program needn't handle non-finite values.
Results may differ from a plain program's by a relative error of at most 0.004.
Values may be sent and summed in bfloat16 or wider, within the bound.
A program may use at most 128 MiB of HBM per device.

v0:
```python
import jax
import jax.numpy as jnp
from jax import lax
from jax.sharding import PartitionSpec as P


def padded_2(block, sides, width):
    for axis, dim in sides:
        count = lax.axis_size(axis)
        forward = [(i, i + 1) for i in range(count - 1)]
        backward = [(target, source) for source, target in forward]
        low = lax.ppermute(
            lax.slice_in_dim(block, block.shape[dim] - width, None, axis=dim), axis, forward
        )
        high = lax.ppermute(lax.slice_in_dim(block, 0, width, axis=dim), axis, backward)
        block = jnp.concatenate([low, block, high], axis=dim)
    return block


def smooth_block(padded, weights):
    center = padded[1:-1, 1:-1]
    along_x = padded[2:, 1:-1] + padded[:-2, 1:-1]
    along_y = padded[1:-1, 2:] + padded[1:-1, :-2]
    zpad = jnp.pad(center, ((0, 0), (0, 0), (1, 1), (0, 0)))
    along_z = zpad[:, :, 2:] + zpad[:, :, :-2]
    twice = 2.0 * center
    return (
        center
        + weights[..., 0:1] * (along_x - twice)
        + weights[..., 1:2] * (along_y - twice)
        + weights[..., 2:3] * (along_z - twice)
    )


def filter_norm(smoothed, taps):
    count = taps.shape[0]
    half = (count - 1) // 2
    frames = smoothed.shape[-1]
    padded = jnp.pad(smoothed, ((0, 0), (0, 0), (0, 0), (half, half)))
    filtered = jnp.zeros_like(smoothed)
    for step in range(count):
        filtered = filtered + taps[step] * padded[..., step : step + frames]
    centered = filtered - jnp.mean(filtered, axis=-1, keepdims=True)
    scale = lax.rsqrt(jnp.mean(centered * centered, axis=-1, keepdims=True) + 1e-05)
    return (centered * scale).astype(jnp.bfloat16)


def lookup(width_class, kernel):
    weights = jnp.zeros(width_class.shape + (3,), jnp.float32)
    for klass in range(kernel.shape[1]):
        hit = (width_class == klass).astype(jnp.float32)[..., None]
        weights = weights + hit * kernel[:, klass]
    return weights


def tile_of(left, right, inverse):
    product = lax.dot_general(
        left, right, (((1,), (1,)), ((), ())), preferred_element_type=jnp.float32
    )
    return (product * inverse).astype(jnp.bfloat16)


def local(signal, width_class, kernel, taps, chosen):
    padded = padded_2(signal, (("loop", 1), ("slab", 0)), 1)
    weights = lookup(width_class, kernel)
    zscored = filter_norm(smooth_block(padded.astype(jnp.float32), weights), taps)
    frames = zscored.shape[-1]
    flat = zscored.reshape(-1, frames)
    rows = jnp.take(flat, chosen.reshape(-1), axis=0)
    panel = lax.all_to_all(rows, "slab", split_axis=0, concat_axis=0, tiled=True)
    inverse = 1.0 / frames**0.5
    height = panel.shape[0]
    wide = tile_of(panel, lax.all_gather(panel, "loop", axis=0, tiled=True), inverse)
    return wide.reshape(height, 1, wide.shape[1])


def solution(mesh):
    in_specs = (
        P("slab", "loop", None, None),
        P("slab", "loop", None),
        P(),
        P(),
        P("loop", "slab", None),
    )
    out_specs = P("loop", "slab", None)
    return jax.shard_map(local, mesh=mesh, in_specs=in_specs, out_specs=out_specs, check_vma=False)
```

profile of v0, /device:TPU:1, one launch (start us, length us, event | category | flops | bytes accessed | tf_op | source)
XLA Modules:
  0.0 405.2 jit_solution(7328015001622252645)
XLA Ops:
  6.5 1.8 fusion.18
  8.3 4.9 %collective-permute-start = (bf16[4,1,64,1920]{3,2,1,0:T(8,128)(2,1)S(1)}, bf16[4,1,64,1920]{3,2,1,0:T(8,128)(2,1)S(1)}, u32[]{:S(2)}, u32[]{:S(2)}) collective-permute-start(bf16[4,1,64,1920]{3,2,1,0:T(8,128)(2,1)S(1)} %get-tuple-element.14), channel_id=1, source_target_pairs={{0,8},{8,16},{16,24},{24,32},{32,40},{40,48},{48,56},{56,64},{64,7... | collective-permute-start | bytes 2949128 | tf_op jit(solution)/shard_map/ppermute | solution.py:12
  13.3 1.9 collective-permute-start.1
  15.2 9.1 %collective-permute-done = bf16[4,1,64,1920]{3,2,1,0:T(8,128)(2,1)S(1)} collective-permute-done((bf16[4,1,64,1920]{3,2,1,0:T(8,128)(2,1)S(1)}, bf16[4,1,64,1920]{3,2,1,0:T(8,128)(2,1)S(1)}, u32[]{:S(2)}, u32[]{:S(2)}) %collective-permute-start) | collective-permute-done | bytes 983072 | tf_op jit(solution)/shard_map/ppermute | solution.py:12
  24.4 0.6 constant_dynamic-update-slice_fusion.1
  25.0 3.7 collective-permute-done.1
  28.8 2.6 copy-done
  31.4 1.4 fusion.17
  32.8 5.0 %collective-permute-start.2 = (bf16[1,6,64,1920]{3,2,1,0:T(8,128)(2,1)}, bf16[1,6,64,1920]{3,2,1,0:T(8,128)(2,1)S(1)}, u32[]{:S(2)}, u32[]{:S(2)}) collective-permute-start(bf16[1,6,64,1920]{3,2,1,0:T(8,128)(2,1)} %get-tuple-element.11), channel_id=1, source_target_pairs={{0,1},{1,2},{2,3},{3,4},{4,5},{5,6},{6,7},{8,9},{9,10},{10,11},{11... | collective-permute-start | bytes 4423688 | tf_op jit(solution)/shard_map/ppermute | solution.py:12
  37.8 1.3 collective-permute-start.3
  39.6 0.6 reduce.11
  40.5 0.7 fusion.19
  41.4 18.0 %collective-permute-done.2 = bf16[1,6,64,1920]{3,2,1,0:T(8,128)(2,1)S(1)} collective-permute-done((bf16[1,6,64,1920]{3,2,1,0:T(8,128)(2,1)}, bf16[1,6,64,1920]{3,2,1,0:T(8,128)(2,1)S(1)}, u32[]{:S(2)}, u32[]{:S(2)}) %collective-permute-start.2) | collective-permute-done | bytes 1474592 | tf_op jit(solution)/shard_map/ppermute | solution.py:12
  59.3 33.3 %collective-permute-done.3 = bf16[1,6,64,1920]{3,2,1,0:T(8,128)(2,1)} collective-permute-done((bf16[1,6,64,1920]{3,2,1,0:T(8,128)(2,1)S(1)}, bf16[1,6,64,1920]{3,2,1,0:T(8,128)(2,1)}, u32[]{:S(2)}, u32[]{:S(2)}) %collective-permute-start.3) | collective-permute-done | bytes 1474592 | tf_op jit(solution)/shard_map/ppermute | solution.py:15
  92.6 4.4 %maximum_convert_fusion = f32[6,6,64,1920]{3,2,1,0:T(8,128)S(1)} fusion(bf16[1,6,64,1920]{3,2,1,0:T(8,128)(2,1)} %collective-permute-done.3, bf16[4,6,64,1920]{3,2,1,0:T(8,128)(2,1)} %copy-done, bf16[1,6,64,1920]{3,2,1,0:T(8,128)(2,1)S(1)} %collective-permute-done.2), kind=kLoop, calls=%fused_computation.3 | loop fusion | flops 13271040 | bytes 26542080 | tf_op jit(solution)/shard_map/convert_element_type | solution.py:66
  97.0 3.9 slice.145
  100.8 14.9 %fusion.4 = f32[4,4,64,1920]{3,2,1,0:T(8,128)} fusion(f32[4,4,64,1920]{3,2,1,0:T(8,128)} %slice.145, f32[6,6,64,1920]{3,2,1,0:T(8,128)S(1)} %maximum_convert_fusion, f32[4,4,64]{2,1,0:T(4,128)S(1)} %get-tuple-element.16, f32[4,4,64]{2,1,0:T(4,128)S(1)} %get-tuple-element.17, f32[4,4,64]{2,1,0:T(4,128)S(1)} %get-tuple-element.15), kind=kLoop, calls=%fused_computation.9 | loop fusion | flops 25559040 | bytes 47198208 | tf_op jit(solution)/shard_map/add | solution.py:28
  115.8 44.5 %fusion.16 = (f32[4,4,64]{2,1,0:T(4,128)S(1)}, f32[4,4,64,1920]{3,2,1,0:T(8,128)S(1)}) fusion(f32[]{:T(128)} %bitcast.11, f32[]{:T(128)} %bitcast.10, f32[]{:T(128)} %bitcast.9, f32[]{:T(128)} %bitcast.8, f32[4,4,64,1920]{3,2,1,0:T(8,128)} %fusion.4, f32[]{:T(128)} %bitcast.7, f32[]{:T(128)} %bitcast.6, f32[]{:T(128)} %bitcast.5, f32[]{:T(128)} %bitcast.4, ...), kind=kLoop, calls=%fused_computation.51 | loop fusion | flops 35388416 | bytes 15732772 | tf_op jit(solution)/shard_map/reduce_sum | solution.py:43
  160.3 0.9 multiply_reduce_fusion
  161.3 2.8 multiply_convert_fusion.1
  164.0 6.9 %gather_fusion = bf16[512,1920]{1,0:T(8,128)(2,1)S(1)} fusion(bf16[1024,1920]{1,0:T(8,128)(2,1)} %bitcast.25, s32[1024]{0:T(1024)S(1)} %pad_clamp_fusion), kind=kCustom, calls=%fused_computation | custom fusion | bytes 3934208 | tf_op jit(solution)/shard_map/jit(_take)/gather | solution.py:69
  171.2 24.3 %all_to_all.9 = bf16[8,64,1920]{2,1,0:T(8,128)(2,1)} all-to-all(bf16[8,64,1920]{2,1,0:T(8,128)(2,1)S(1)} %broadcast_select_fusion), channel_id=1, replica_groups=mesh['loop'=16,'slab'=8] {'slab'}, dimensions={0} | all-to-all | bytes 3932160 | tf_op jit(solution)/shard_map/all_to_all | solution.py:70
  195.5 178.2 %all-gather.2.cloned.1.call-done = bf16[8192,1920]{1,0:T(8,128)(2,1)} async-done(((bf16[512,1920]{1,0:T(8,128)(2,1)}), bf16[8192,1920]{1,0:T(8,128)(2,1)}) %all-gather.2.cloned.1.call-update) | async-done | bytes 31457296 | tf_op jit(solution)/shard_map/all_gather | solution.py:73
  373.7 24.6 %fusion = bf16[512,1,8192]{2,0,1:T(8,128)(2,1)} fusion(bf16[512,1920]{1,0:T(8,128)(2,1)} %bitcast.27, bf16[8192,1920]{1,0:T(8,128)(2,1)} %all-gather.2.cloned.1.call-done), kind=kOutput, calls=%fused_computation.2 | convolution fusion | flops 16114515968 | bytes 41811968 | tf_op jit(solution)/shard_map/dot_general | solution.py:57
  (27 shorter events, 1.5 us)
Async XLA Ops:
  6.5 367.2 %all-gather.2.cloned.1.call-start = ((), (), s32[]{:S(2)}) async-start(), calls=%async_computation.1 | async-start | bytes 33423360 | tf_op jit(solution)/shard_map/all_gather | solution.py:73
  6.5 17.8 %copy-start.1 = (bf16[4,4,64,1920]{3,2,1,0:T(8,128)(2,1)S(1)}, bf16[4,4,64,1920]{3,2,1,0:T(8,128)(2,1)}, u32[]{:S(2)}) copy-start(bf16[4,4,64,1920]{3,2,1,0:T(8,128)(2,1)} %param.5) | copy-start | bytes 11796484
  8.3 16.0 %collective-permute-start = (bf16[4,1,64,1920]{3,2,1,0:T(8,128)(2,1)S(1)}, bf16[4,1,64,1920]{3,2,1,0:T(8,128)(2,1)S(1)}, u32[]{:S(2)}, u32[]{:S(2)}) collective-permute-start(bf16[4,1,64,1920]{3,2,1,0:T(8,128)(2,1)S(1)} %get-tuple-element.14), channel_id=1, source_target_pairs={{0,8},{8,16},{16,24},{24,32},{32,40},{40,48},{48,56},{56,64},{64,7... | collective-permute-start | bytes 2949128 | tf_op jit(solution)/shard_map/ppermute | solution.py:12
  13.3 15.4 %collective-permute-start.1 = (bf16[4,1,64,1920]{3,2,1,0:T(8,128)(2,1)S(1)}, bf16[4,1,64,1920]{3,2,1,0:T(8,128)(2,1)S(1)}, u32[]{:S(2)}, u32[]{:S(2)}) collective-permute-start(bf16[4,1,64,1920]{3,2,1,0:T(8,128)(2,1)S(1)} %get-tuple-element.13), channel_id=1, source_target_pairs={{8,0},{16,8},{24,16},{32,24},{40,32},{48,40},{56,48},{64,56},{72,6... | collective-permute-start | bytes 2949128 | tf_op jit(solution)/shard_map/ppermute | solution.py:15
  24.4 15.2 %copy-start.5 = (s32[1,1,512]{2,1,0:T(1,128)S(1)}, s32[1,1,512]{2,1,0:T(1,128)}, u32[]{:S(2)}) copy-start(s32[1,1,512]{2,1,0:T(1,128)} %param.9) | copy-start | bytes 6148
  24.4 15.9 %copy-start.3 = (f32[3,4]{1,0:T(4,128)S(1)}, f32[3,4]{1,0:T(4,128)}, u32[]{:S(2)}) copy-start(f32[3,4]{1,0:T(4,128)} %param.7) | copy-start | bytes 148
  24.4 16.1 %copy-start.2 = (f32[9]{0:T(128)S(1)}, f32[9]{0:T(128)}, u32[]{:S(2)}) copy-start(f32[9]{0:T(128)} %param.8) | copy-start | bytes 112
  24.4 16.8 %copy-start.4 = (s32[4,4,64]{2,1,0:T(4,128)S(1)}, s32[4,4,64]{2,1,0:T(4,128)}, u32[]{:S(2)}) copy-start(s32[4,4,64]{2,1,0:T(4,128)} %param.6) | copy-start | bytes 12292
  28.8 2.6 copy-start
  32.8 26.6 %collective-permute-start.2 = (bf16[1,6,64,1920]{3,2,1,0:T(8,128)(2,1)}, bf16[1,6,64,1920]{3,2,1,0:T(8,128)(2,1)S(1)}, u32[]{:S(2)}, u32[]{:S(2)}) collective-permute-start(bf16[1,6,64,1920]{3,2,1,0:T(8,128)(2,1)} %get-tuple-element.11), channel_id=1, source_target_pairs={{0,1},{1,2},{2,3},{3,4},{4,5},{5,6},{6,7},{8,9},{9,10},{10,11},{11... | collective-permute-start | bytes 4423688 | tf_op jit(solution)/shard_map/ppermute | solution.py:12
  37.8 54.8 %collective-permute-start.3 = (bf16[1,6,64,1920]{3,2,1,0:T(8,128)(2,1)S(1)}, bf16[1,6,64,1920]{3,2,1,0:T(8,128)(2,1)}, u32[]{:S(2)}, u32[]{:S(2)}) collective-permute-start(bf16[1,6,64,1920]{3,2,1,0:T(8,128)(2,1)S(1)} %get-tuple-element.12), channel_id=1, source_target_pairs={{1,0},{2,1},{3,2},{4,3},{5,4},{6,5},{7,6},{9,8},{10,9},{11,10},{12... | collective-permute-start | bytes 4423688 | tf_op jit(solution)/shard_map/ppermute | solution.py:15
Sparse Core Ops, SparseCore 0:
  195.6 178.0 all-gather.1
where the time goes:
time: 406 us; the launch traced here: 405 us
  waiting for transfers between devices  242 us (60%)
  other arithmetic  68.5 us (17%)
  matrix products  24.6 us (6%)
  blocking collectives  24.3 us (6%)
  local copies, waits for them, and re-layouts  18.7 us (5%)
  between operations  13.6 us (3%)
  starting transfers between devices  13.2 us (3%)
    all_gather x1, waiting for transfers between devices, local(): lax.all_gather(panel, 'loop', axis=0, tiled=True)  178 us
    reduce_sum x1, other arithmetic, filter_norm(): centered = filtered - jnp.mean(filtered, axis=-1, keepdims=True)  44.5 us
    ppermute x2, waiting for transfers between devices, padded_2(): lax.ppermute(lax.slice_in_dim(block, 0, width, axis=dim), axis, backward)  37 us
    ppermute x2, waiting for transfers between devices, padded_2(): lax.ppermute(lax.slice_in_dim(block, block.shape[dim] - width, None, axis...  27.1 us
    dot_general x1, matrix products, tile_of(): lax.dot_general(left, right, (((1,), (1,)), ((), ())), preferred_element_...  24.6 us
    all_to_all x1, blocking collectives, local(): lax.all_to_all(rows, 'slab', split_axis=0, concat_axis=0, tiled=True)  24.3 us
    add x1, other arithmetic, smooth_block(): center + weights[..., 0:1] * (along_x - twice)  14.9 us
    ppermute x2, starting transfers between devices, padded_2(): lax.ppermute(lax.slice_in_dim(block, block.shape[dim] - width, None, axis...  9.96 us
  transfers between devices with their start and end apart: 5, of which 5 were waited for; matrix products, arithmetic and copies ran while one was open for 1% of the time, Pallas kernels for 0%

commit v1 on v0

v1 whole, which is shorter than its diff:
```python
import functools

import jax
import jax.numpy as jnp
from jax import lax
from jax.experimental import pallas as pl
from jax.experimental.pallas import tpu as pltpu
from jax.sharding import PartitionSpec as P

MESH = pl.DeviceIdType.MESH
CX, CY, CZ, FRAMES = 4, 4, 64, 1920
VOXELS = CX * CY * CZ
PANEL = 512
SHARE = 64
N_LOOP, N_SLAB = 16, 8
CHUNK = 384
CHUNKS = FRAMES // CHUNK
ORDER = (0, 1, 3, 2)


def front_kernel(sig, chosen, wclass, kernel, taps, rows, block, halo, vox, w_hi, w_lo, smooth, filt, load_sem, send_sem, recv_sem):
    loop, slab = lax.axis_index("loop"), lax.axis_index("slab")
    has = (slab > 0, slab < N_SLAB - 1, loop > 0, loop < N_LOOP - 1)
    peers = ((loop, slab - 1), (loop, slab + 1), (loop - 1, slab), (loop + 1, slab))
    planes = (sig.at[0], sig.at[CX - 1], sig.at[:, 0], sig.at[:, CY - 1])
    lands = (1, 0, 3, 2)

    barrier = pltpu.get_barrier_semaphore()
    for there, peer in zip(has, peers):
        @pl.when(there)
        def _():
            pl.semaphore_signal(barrier, inc=1, device_id=peer, device_id_type=MESH)
    load = pltpu.make_async_copy(sig, block, load_sem)
    load.start()
    pl.semaphore_wait(barrier, sum(there.astype(jnp.int32) for there in has))

    def halo_copy(d, k):
        lanes = pl.ds(k * CHUNK, CHUNK)
        return pltpu.make_async_remote_copy(
            src_ref=planes[d].at[:, :, lanes],
            dst_ref=halo.at[lands[d], :, :, lanes],
            send_sem=send_sem.at[d, k],
            recv_sem=recv_sem.at[lands[d], k],
            device_id=peers[d],
            device_id_type=MESH,
        )

    def halo_wait(d, k):
        lanes = pl.ds(k * CHUNK, CHUNK)
        pltpu.make_async_remote_copy(
            src_ref=halo.at[d, :, :, lanes],
            dst_ref=halo.at[d, :, :, lanes],
            send_sem=send_sem.at[d, k],
            recv_sem=recv_sem.at[d, k],
            device_id=peers[d],
            device_id_type=MESH,
        ).wait_recv()

    for k in range(CHUNKS):
        for d in range(4):
            @pl.when(has[d])
            def _():
                halo_copy(d, k).start()

    for d in range(4):
        @pl.when(jnp.logical_not(has[d]))
        def _():
            halo[d] = jnp.zeros_like(halo[d])
    pad = jnp.zeros((PANEL, 128), jnp.float32)
    smooth[:, 0:128] = pad
    smooth[:, 128 + FRAMES :] = pad

    index = jnp.broadcast_to(chosen[...].astype(jnp.float32), (128, PANEL))
    vox[...] = jnp.transpose(index).astype(jnp.int32)
    tall = 64

    def build(t, _):
        at = pl.ds(pl.multiple_of(t * tall, tall), tall)
        v = vox[at, :]
        iota = lax.broadcasted_iota(jnp.int32, (tall, 128), 1)
        iota_z = lax.broadcasted_iota(jnp.int32, (tall, CZ), 1)
        hits = jnp.zeros((tall, CZ), jnp.int32)
        for run in range(CX * CY):
            hits = hits + jnp.where(v[:, :CZ] == iota_z + run * CZ, wclass[run : run + 1, :], 0)
        klass = jnp.sum(hits.astype(jnp.float32), axis=1, keepdims=True)
        weight = []
        for d in range(3):
            w = jnp.zeros_like(klass)
            for c in range(4):
                w = w + jnp.where(klass == float(c), kernel[d, c], 0.0)
            weight.append(jnp.broadcast_to(w, (tall, 128)))
        wx, wy, wz = weight
        centre = 1.0 - 2.0 * (wx + wy + wz)
        x, y, z = v >> 8, (v >> 6) & 3, v & 63
        none = jnp.full_like(v, -1)
        y_lo, y_hi = jnp.where(y > 0, v - CZ, none), jnp.where(y < CY - 1, v + CZ, none)
        z_lo, z_hi = jnp.where(z > 0, v - 1, none), jnp.where(z < CZ - 1, v + 1, none)
        plane = x * CZ + z

        def put(column, w):
            hi = w.astype(jnp.bfloat16)
            w_hi[at, column : column + 128] = hi
            w_lo[at, column : column + 128] = (w - hi.astype(jnp.float32)).astype(jnp.bfloat16)

        zero = jnp.zeros((tall, 128), jnp.float32)
        for b in range(VOXELS // 128):
            col = iota + b * 128
            w = jnp.where(col == v, centre, zero)
            w = jnp.where((col == v - 256) | (col == v + 256), wx, w)
            w = jnp.where((col == y_lo) | (col == y_hi), wy, w)
            put(b * 128, jnp.where((col == z_lo) | (col == z_hi), wz, w))
        picks = (
            (v, wx),
            (v - 768, wx),
            (jnp.where(y == 0, plane, none), wy),
            (jnp.where(y == CY - 1, plane, none), wy),
        )
        for d, (pick, w) in enumerate(picks):
            for b in range(2):
                put(VOXELS + d * 256 + b * 128, jnp.where(iota + b * 128 == pick, w, zero))
        return 0

    lax.fori_loop(0, PANEL // tall, build, 0)

    half = 256

    def product(ref, first, k, h):
        at = pl.ds(pl.multiple_of(h * half, half), half)
        lanes = pl.ds(pl.multiple_of(k * CHUNK, 128), CHUNK)
        right = ref[:, :, :, lanes].reshape(VOXELS, CHUNK)
        cols = pl.ds(first, VOXELS)
        return jnp.dot(w_hi[at, cols], right, preferred_element_type=jnp.float32) + jnp.dot(
            w_lo[at, cols], right, preferred_element_type=jnp.float32
        )

    load.wait()

    def inner(i, _):
        k, h = i // 2, i % 2
        at = pl.ds(pl.multiple_of(h * half, half), half)
        smooth[at, pl.ds(pl.multiple_of(128 + k * CHUNK, 128), CHUNK)] = product(block, 0, k, h)
        return 0

    lax.fori_loop(0, CHUNKS * 2, inner, 0)

    def filter_part(first, width):
        def body(t, _):
            at = pl.ds(pl.multiple_of(t * 16, 16), 16)
            window = smooth[at, pl.ds(first, width + 256)]
            total = None
            for tap in range(9):
                shift = 4 - tap
                moved = window if shift == 0 else pltpu.roll(window, shift % (width + 256), axis=1)
                term = taps[tap] * moved[:, 128 : 128 + width]
                total = term if total is None else total + term
            filt[at, pl.ds(first, width)] = total
            return 0

        lax.fori_loop(0, PANEL // 16, body, 0)

    for k in range(CHUNKS):
        for d in range(4):
            @pl.when(has[d])
            def _():
                halo_wait(d, k)

        def outer(h, _):
            at = pl.ds(pl.multiple_of(h * half, half), half)
            smooth[at, 128 + k * CHUNK : 128 + (k + 1) * CHUNK] += product(halo, VOXELS, k, h)
            return 0

        lax.fori_loop(0, 2, outer, 0)
        first = max(0, k * CHUNK - 128)
        last = FRAMES if k == CHUNKS - 1 else (k + 1) * CHUNK - 128
        filter_part(first, last - first)

    def norm(t, _):
        at = pl.ds(pl.multiple_of(t * 16, 16), 16)
        f = filt[at, :]
        centred = f - jnp.mean(f, axis=1, keepdims=True)
        scale = lax.rsqrt(jnp.mean(centred * centred, axis=1, keepdims=True) + 1e-05)
        rows[at, :] = (centred * scale).astype(jnp.bfloat16)
        return 0

    lax.fori_loop(0, PANEL // 16, norm, 0)

    for k in range(CHUNKS):
        for d in range(4):
            @pl.when(has[d])
            def _():
                halo_copy(d, k).wait_send()


def front(signal, chosen, wclass, kernel, taps):
    vmem = pl.BlockSpec(memory_space=pltpu.VMEM)
    smem = pl.BlockSpec(memory_space=pltpu.SMEM)
    return pl.pallas_call(
        front_kernel,
        out_shape=jax.ShapeDtypeStruct((PANEL, FRAMES), jnp.bfloat16),
        in_specs=[pl.BlockSpec(memory_space=pl.ANY), vmem, vmem, smem, smem],
        out_specs=vmem,
        scratch_shapes=[
            pltpu.VMEM((CX, CY, CZ, FRAMES), jnp.bfloat16),
            pltpu.VMEM((4, 4, CZ, FRAMES), jnp.bfloat16),
            pltpu.VMEM((PANEL, 128), jnp.int32),
            pltpu.VMEM((PANEL, 2 * VOXELS), jnp.bfloat16),
            pltpu.VMEM((PANEL, 2 * VOXELS), jnp.bfloat16),
            pltpu.VMEM((PANEL, FRAMES + 256), jnp.float32),
            pltpu.VMEM((PANEL, FRAMES), jnp.float32),
            pltpu.SemaphoreType.DMA,
            pltpu.SemaphoreType.DMA((4, CHUNKS)),
            pltpu.SemaphoreType.DMA((4, CHUNKS)),
        ],
        compiler_params=pltpu.CompilerParams(
            collective_id=0, has_side_effects=True, vmem_limit_bytes=56 * 2**20
        ),
        name="front",
    )(signal, chosen, wclass, kernel, taps)


def group_kernel(rows, tiles, held, stage, own_sem, swap_sem, x_sem, up_sem, down_sem, core_sem, recv_sem, out_sem):
    loop, slab = lax.axis_index("loop"), lax.axis_index("slab")
    x, z, c = loop // 8, (loop // 2) % 4, loop % 2
    y, h = slab // 2, slab % 2
    z_up, z_down, z_far = (z + 1) % 4, (z + 3) % 4, (z + 2) % 4

    def panel(px, pz, pc=None):
        return px * 8 + pz * 2 + (c if pc is None else pc)

    up, down = (panel(x, z_up), slab), (panel(x, z_down), slab)
    across, sibling = (panel(1 - x, z), slab), (panel(x, z, 1 - c), slab)
    inside = [(loop, ((y + dy) % 4) * 2 + h) for dy in (1, 3, 2)]
    outside = [(panel(1 - x, z), ((y + dy) % 4) * 2 + 1 - h) for dy in ORDER]

    barrier = pltpu.get_barrier_semaphore()
    peers = [up, down, across, sibling] + inside + outside
    for peer in peers:
        pl.semaphore_signal(barrier, inc=1, device_id=peer, device_id_type=MESH)
    pl.semaphore_wait(barrier, len(peers))

    def at(p):
        dy = jnp.where(p == 2, 3, jnp.where(p == 3, 2, p))
        return (y + dy) % 4

    def copy(q, py, ph, sem, peer):
        return pltpu.make_async_remote_copy(
            src_ref=held.at[q, py, ph],
            dst_ref=held.at[q, py, ph],
            send_sem=sem.at[q, py, ph],
            recv_sem=recv_sem.at[q, py, ph],
            device_id=peer,
            device_id_type=MESH,
        )

    def arrived(q, py, ph):
        copy(q, py, ph, core_sem, sibling).wait_recv()

    swaps = []
    for i, peer in enumerate(outside + inside):
        to_y, to_h = peer[1] // 2, peer[1] % 2
        swaps.append(pltpu.make_async_remote_copy(
            src_ref=rows.at[to_y, to_h],
            dst_ref=held.at[loop, y, h],
            send_sem=swap_sem.at[i],
            recv_sem=recv_sem.at[loop, y, h],
            device_id=peer,
            device_id_type=MESH,
        ))
    pltpu.make_async_copy(rows.at[y, h], held.at[loop, y, h], recv_sem.at[loop, y, h]).start()
    for i in (0, 4, 1, 5, 2, 6, 3):
        swaps[i].start()

    mine, other = panel(x, z), panel(1 - x, z)

    def begin(p, _):
        py = at(p)

        @pl.when(p == 0)
        def _():
            pltpu.make_async_copy(rows.at[y, h], held.at[loop, y, h], recv_sem.at[loop, y, h]).wait()

        @pl.when(p > 0)
        def _():
            arrived(mine, py, h)
        copy(mine, py, h, up_sem, up).start()
        copy(mine, py, h, down_sem, down).start()
        copy(mine, py, h, x_sem, across).start()
        copy(mine, py, h, core_sem, sibling).start()
        arrived(other, py, 1 - h)
        copy(other, py, 1 - h, x_sem, across).start()
        copy(other, py, 1 - h, up_sem, up).start()
        copy(other, py, 1 - h, down_sem, down).start()
        copy(other, py, 1 - h, core_sem, sibling).start()
        return 0

    lax.fori_loop(0, 4, begin, 0)

    def second(p, _):
        py = at(p)
        even = p % 2 == 0
        for pz, sem, peer, on in ((z_down, up_sem, up, even), (z_up, down_sem, down, jnp.logical_not(even))):
            for px, ph in ((x, h), (1 - x, 1 - h)):
                q = panel(px, pz)
                arrived(q, py, ph)

                @pl.when(on)
                def _():
                    copy(q, py, ph, sem, peer).start()
                if px is x:
                    copy(q, py, ph, x_sem, across).start()
                copy(q, py, ph, core_sem, sibling).start()
        arrived(mine, py, 1 - h)
        copy(mine, py, 1 - h, up_sem, up).start()
        copy(mine, py, 1 - h, down_sem, down).start()
        copy(mine, py, 1 - h, core_sem, sibling).start()
        arrived(other, py, h)
        copy(other, py, h, core_sem, sibling).start()
        return 0

    lax.fori_loop(0, 4, second, 0)

    def from_sibling(px, pz):
        def body(i, _):
            arrived(panel(px, pz, 1 - c), i // 2, i % 2)
            return 0

        lax.fori_loop(0, 8, body, 0)

    def tile(q):
        left = held[loop].reshape(PANEL, FRAMES)
        for j in range(2):
            right = held[q, 2 * j : 2 * j + 2].reshape(PANEL // 2, FRAMES)
            product = lax.dot_general(left, right, (((1,), (1,)), ((), ())), preferred_element_type=jnp.float32)
            stage[q, :, j * 256 : (j + 1) * 256] = (product * (1.0 / FRAMES**0.5)).astype(jnp.bfloat16)
        tile_copy(q).start()

    def tile_copy(q):
        return pltpu.make_async_copy(
            stage.at[q], tiles.at[:, pl.ds(pl.multiple_of(q * PANEL, PANEL), PANEL)], out_sem.at[q]
        )

    def both(px, pz):
        from_sibling(px, pz)

        def body(pc, _):
            tile(panel(px, pz, pc))
            return 0

        lax.fori_loop(0, 2, body, 0)

    def third(p, _):
        py = at(p)
        q = panel(x, z_far)
        arrived(q, py, h)
        copy(q, py, h, x_sem, across).start()
        copy(q, py, h, core_sem, sibling).start()
        even = p % 2 == 0
        for pz, sem, peer, on in ((z_down, up_sem, up, even), (z_up, down_sem, down, jnp.logical_not(even))):
            q = panel(x, pz)
            arrived(q, py, 1 - h)

            @pl.when(on)
            def _():
                copy(q, py, 1 - h, sem, peer).start()
            copy(q, py, 1 - h, core_sem, sibling).start()
        q = panel(1 - x, z_far)
        arrived(q, py, 1 - h)
        copy(q, py, 1 - h, core_sem, sibling).start()
        return 0

    lax.fori_loop(0, 4, third, 0)

    def near(i, _):
        both(jnp.where(i == 0, x, 1 - x), z)
        return 0

    lax.fori_loop(0, 2, near, 0)

    def fourth(p, _):
        py = at(p)
        for pz in (z_down, z_up):
            q = panel(1 - x, pz)
            arrived(q, py, h)
            copy(q, py, h, core_sem, sibling).start()
        return 0

    lax.fori_loop(0, 4, fourth, 0)

    def beside(i, _):
        both(x, jnp.where(i == 0, z_down, z_up))
        return 0

    lax.fori_loop(0, 2, beside, 0)

    def fifth(p, _):
        py = at(p)
        q = panel(x, z_far)
        arrived(q, py, 1 - h)
        copy(q, py, 1 - h, core_sem, sibling).start()
        return 0

    lax.fori_loop(0, 4, fifth, 0)

    def beyond(i, _):
        both(jnp.where(i == 2, x, 1 - x), jnp.where(i == 0, z_down, jnp.where(i == 1, z_up, z_far)))
        return 0

    lax.fori_loop(0, 3, beyond, 0)

    def sixth(p, _):
        py = at(p)
        q = panel(1 - x, z_far)
        arrived(q, py, h)
        copy(q, py, h, core_sem, sibling).start()
        return 0

    lax.fori_loop(0, 4, sixth, 0)
    both(1 - x, z_far)

    for swap in swaps:
        swap.wait_send()

    def left(p, _):
        py = at(p)
        even = p % 2 == 0
        for pz in range(4):
            q = panel(x, pz)
            copy(q, py, h, x_sem, across).wait_send()
            for px in range(2):
                for ph in range(2):
                    copy(panel(px, pz), py, ph, core_sem, sibling).wait_send()
        copy(other, py, 1 - h, x_sem, across).wait_send()
        for q, ph in ((mine, h), (other, 1 - h), (mine, 1 - h)):
            copy(q, py, ph, up_sem, up).wait_send()
            copy(q, py, ph, down_sem, down).wait_send()
        for px, ph in ((x, h), (1 - x, 1 - h), (x, 1 - h)):
            @pl.when(even)
            def _():
                copy(panel(px, z_down), py, ph, up_sem, up).wait_send()

            @pl.when(jnp.logical_not(even))
            def _():
                copy(panel(px, z_up), py, ph, down_sem, down).wait_send()
        return 0

    lax.fori_loop(0, 4, left, 0)

    def written(q, _):
        tile_copy(q).wait()
        return 0

    lax.fori_loop(0, N_LOOP, written, 0)


def group(rows):
    block = (N_LOOP, 4, 2)
    return pl.pallas_call(
        group_kernel,
        out_shape=jax.ShapeDtypeStruct((PANEL, N_LOOP * PANEL), jnp.bfloat16),
        in_specs=[pl.BlockSpec(memory_space=pltpu.VMEM)],
        out_specs=pl.BlockSpec(memory_space=pl.ANY),
        scratch_shapes=[
            pltpu.VMEM(block + (SHARE, FRAMES), jnp.bfloat16),
            pltpu.VMEM((N_LOOP, PANEL, PANEL), jnp.bfloat16),
            pltpu.SemaphoreType.DMA,
            pltpu.SemaphoreType.DMA((7,)),
            pltpu.SemaphoreType.DMA(block),
            pltpu.SemaphoreType.DMA(block),
            pltpu.SemaphoreType.DMA(block),
            pltpu.SemaphoreType.DMA(block),
            pltpu.SemaphoreType.DMA(block),
            pltpu.SemaphoreType.DMA((N_LOOP,)),
        ],
        compiler_params=pltpu.CompilerParams(
            collective_id=1, has_side_effects=True, vmem_limit_bytes=56 * 2**20
        ),
        name="group",
    )(rows)


def local(signal, width_class, kernel, taps, chosen):
    rows = front(signal, chosen.reshape(1, PANEL), width_class.reshape(CX * CY, CZ), kernel, taps)
    wide = group(rows.reshape(4, 2, SHARE, FRAMES))
    return wide.reshape(PANEL, 1, N_LOOP * PANEL)


def solution(mesh):
    in_specs = (
        P("slab", "loop", None, None),
        P("slab", "loop", None),
        P(),
        P(),
        P("loop", "slab", None),
    )
    return jax.shard_map(local, mesh=mesh, in_specs=in_specs, out_specs=P("loop", "slab", None), check_vma=False)
```

time: 406 us -> 211 us (0.52)
  waiting for transfers between devices: 242 us -> 0 us
  Pallas kernels: 0 us -> 203 us
  other arithmetic: 68.5 us -> 0 us
  matrix products: 24.6 us -> 0 us
  blocking collectives: 24.3 us -> 0 us
  between operations: 13.6 us -> 0.02 us
  starting transfers between devices: 13.2 us -> 0 us
  local copies, waits for them, and re-layouts: 18.7 us -> 7.77 us
    pallas_call x0 -> x2, Pallas kernels: none -> 203 us  [the longest x1 142 us: group(): pl.pallas_call(group_kernel, out_shape=jax.ShapeDtypeStruct((PANEL, N_LOO...]
    all_gather x1 -> x0, waiting for transfers between devices: 178 us -> none  [local(): lax.all_gather(panel, 'loop', axis=0, tiled=True)]
    ppermute x4 -> x0, waiting for transfers between devices: 64 us -> none  [the longest x2 37 us: padded_2(): lax.ppermute(lax.slice_in_dim(block, 0, width, axis=dim), axis, backward)]
    reduce_sum x2 -> x0, other arithmetic: 45.5 us -> none  [the longest x1 44.5 us: filter_norm(): centered = filtered - jnp.mean(filtered, axis=-1, keepdims=True)]
    dot_general x1 -> x0, matrix products: 24.6 us -> none  [tile_of(): lax.dot_general(left, right, (((1,), (1,)), ((), ())), preferred_element_...]
    all_to_all x1 -> x0, blocking collectives: 24.3 us -> none  [local(): lax.all_to_all(rows, 'slab', split_axis=0, concat_axis=0, tiled=True)]
    add x2 -> x0, other arithmetic: 15 us -> none  [the longest x1 14.9 us: smooth_block(): center + weights[..., 0:1] * (along_x - twice)]
    ppermute x4 -> x0, starting transfers between devices: 13.2 us -> none  [the longest x2 9.96 us: padded_2(): lax.ppermute(lax.slice_in_dim(block, block.shape[dim] - width, None, axis...]
  transfers between devices with their start and end apart: 5 -> 0, of which waited for: 5 -> 0; matrix products, arithmetic and copies ran while one was open for 1% -> 0% of each run, Pallas kernels for 0% -> 0%
where the time goes in v1:
time: 211 us; the launch traced here: 210 us
  Pallas kernels  203 us (96%)
  local copies, waits for them, and re-layouts  7.77 us (4%)
    pallas_call x1, Pallas kernels, group(): pl.pallas_call(group_kernel, out_shape=jax.ShapeDtypeStruct((PANEL, N_LOO...  142 us
    pallas_call x1, Pallas kernels, front(): pl.pallas_call(front_kernel, out_shape=jax.ShapeDtypeStruct((PANEL, FRAME...  60.3 us
    unnamed x1, local copies, waits for them, and re-layouts  7.77 us

profile of v1, /device:TPU:1, one launch (start us, length us, event | category | flops | bytes accessed | tf_op | source)
XLA Modules:
  0.0 210.4 jit_solution(6491288357750337371)
XLA Ops:
  0.0 60.3 %front.1 = bf16[512,1920]{1,0:T(8,128)(2,1)} custom-call(bf16[4,4,64,1920]{3,2,1,0:T(8,128)(2,1)} %sig.1, s32[1,512]{1,0:T(1,128)} %bitcast.7, s32[16,64]{1,0:T(8,128)} %bitcast.6, f32[3,4]{1,0:T(4,128)} %kernel.1, f32[9]{0:T(128)} %taps.1), custom_call_target="tpu_custom_call" | custom-call | tf_op jit(solution)/shard_map/front/pallas_call | solution.py:197
  60.3 142.3 %group.1 = bf16[512,8192]{1,0:T(8,128)(2,1)} custom-call(bf16[4,2,64,1920]{3,2,1,0:T(8,128)(2,1)} %bitcast.5), custom_call_target="tpu_custom_call" | custom-call | tf_op jit(solution)/shard_map/group/pallas_call | solution.py:457
  202.6 7.8 %copy.7 = bf16[512,1,8192]{2,0,1:T(8,128)(2,1)} copy(bf16[512,1,8192]{2,0,1:T(8,128)(2,1)} %bitcast.4) | data formatting | bytes 16777216

commit v2 on v1

--- a/solution.py
+++ b/solution.py
@@ -13,12 +13,15 @@
 PANEL = 512
 SHARE = 64
 N_LOOP, N_SLAB = 16, 8
-CHUNK = 384
-CHUNKS = FRAMES // CHUNK
+EDGES = (0, 384, 896, 1408, 1664, 1920)
+CHUNKS = len(EDGES) - 1
+WIDE = 384
+REACH = 128
+FILTER = 256
 ORDER = (0, 1, 3, 2)
 
 
-def front_kernel(sig, chosen, wclass, kernel, taps, rows, block, halo, vox, w_hi, w_lo, smooth, filt, load_sem, send_sem, recv_sem):
+def front_kernel(sig, chosen, wclass, kernel, taps, rows, block, halo, vox, w_hi, w_lo, s_hi, s_lo, t_hi, t_lo, filt, sums, load_sem, send_sem, recv_sem):
     loop, slab = lax.axis_index("loop"), lax.axis_index("slab")
     has = (slab > 0, slab < N_SLAB - 1, loop > 0, loop < N_LOOP - 1)
     peers = ((loop, slab - 1), (loop, slab + 1), (loop - 1, slab), (loop + 1, slab))
@@ -35,7 +38,7 @@
     pl.semaphore_wait(barrier, sum(there.astype(jnp.int32) for there in has))
 
     def halo_copy(d, k):
-        lanes = pl.ds(k * CHUNK, CHUNK)
+        lanes = pl.ds(EDGES[k], EDGES[k + 1] - EDGES[k])
         return pltpu.make_async_remote_copy(
             src_ref=planes[d].at[:, :, lanes],
             dst_ref=halo.at[lands[d], :, :, lanes],
@@ -46,7 +49,7 @@
         )
 
     def halo_wait(d, k):
-        lanes = pl.ds(k * CHUNK, CHUNK)
+        lanes = pl.ds(EDGES[k], EDGES[k + 1] - EDGES[k])
         pltpu.make_async_remote_copy(
             src_ref=halo.at[d, :, :, lanes],
             dst_ref=halo.at[d, :, :, lanes],
@@ -66,9 +69,20 @@
         @pl.when(jnp.logical_not(has[d]))
         def _():
             halo[d] = jnp.zeros_like(halo[d])
-    pad = jnp.zeros((PANEL, 128), jnp.float32)
-    smooth[:, 0:128] = pad
-    smooth[:, 128 + FRAMES :] = pad
+    for part in (s_hi, s_lo):
+        part[:, 0:REACH] = jnp.zeros((PANEL, REACH), jnp.bfloat16)
+        part[:, REACH + FRAMES :] = jnp.zeros((PANEL, REACH), jnp.bfloat16)
+
+    def split(value):
+        hi = value.astype(jnp.bfloat16)
+        return hi, (value - hi.astype(jnp.float32)).astype(jnp.bfloat16)
+
+    wide = FILTER + 2 * REACH
+    lag = lax.broadcasted_iota(jnp.int32, (wide, FILTER), 0) - lax.broadcasted_iota(jnp.int32, (wide, FILTER), 1) - REACH + 4
+    band = jnp.zeros((wide, FILTER), jnp.float32)
+    for tap in range(9):
+        band = jnp.where(lag == tap, taps[tap], band)
+    t_hi[...], t_lo[...] = split(band)
 
     index = jnp.broadcast_to(chosen[...].astype(jnp.float32), (128, PANEL))
     vox[...] = jnp.transpose(index).astype(jnp.int32)
@@ -98,9 +112,7 @@
         plane = x * CZ + z
 
         def put(column, w):
-            hi = w.astype(jnp.bfloat16)
-            w_hi[at, column : column + 128] = hi
-            w_lo[at, column : column + 128] = (w - hi.astype(jnp.float32)).astype(jnp.bfloat16)
+            w_hi[at, column : column + 128], w_lo[at, column : column + 128] = split(w)
 
         zero = jnp.zeros((tall, 128), jnp.float32)
         for b in range(VOXELS // 128):
@@ -124,10 +136,9 @@
 
     half = 256
 
-    def product(ref, first, k, h):
+    def product(ref, first, lanes, h):
         at = pl.ds(pl.multiple_of(h * half, half), half)
-        lanes = pl.ds(pl.multiple_of(k * CHUNK, 128), CHUNK)
-        right = ref[:, :, :, lanes].reshape(VOXELS, CHUNK)
+        right = ref[:, :, :, lanes].reshape(VOXELS, -1)
         cols = pl.ds(first, VOXELS)
         return jnp.dot(w_hi[at, cols], right, preferred_element_type=jnp.float32) + jnp.dot(
             w_lo[at, cols], right, preferred_element_type=jnp.float32
@@ -138,25 +149,25 @@
     def inner(i, _):
         k, h = i // 2, i % 2
         at = pl.ds(pl.multiple_of(h * half, half), half)
-        smooth[at, pl.ds(pl.multiple_of(128 + k * CHUNK, 128), CHUNK)] = product(block, 0, k, h)
-        return 0
-
-    lax.fori_loop(0, CHUNKS * 2, inner, 0)
-
-    def filter_part(first, width):
-        def body(t, _):
-            at = pl.ds(pl.multiple_of(t * 16, 16), 16)
-            window = smooth[at, pl.ds(first, width + 256)]
-            total = None
-            for tap in range(9):
-                shift = 4 - tap
-                moved = window if shift == 0 else pltpu.roll(window, shift % (width + 256), axis=1)
-                term = taps[tap] * moved[:, 128 : 128 + width]
-                total = term if total is None else total + term
-            filt[at, pl.ds(first, width)] = total
-            return 0
-
-        lax.fori_loop(0, PANEL // 16, body, 0)
+        lanes = pl.ds(pl.multiple_of(k * WIDE, 128), WIDE)
+        filt[at, lanes] = product(block, 0, lanes, h)
+        return 0
+
+    lax.fori_loop(0, FRAMES // WIDE * 2, inner, 0)
+    sums[...] = jnp.zeros_like(sums)
+
+    def filter_part(at, first, width):
+        window = pl.ds(first, width + 2 * REACH)
+        hi, lo = s_hi[at, window], s_lo[at, window]
+        rows_of = pl.ds(0, width + 2 * REACH)
+        cols = pl.ds(0, width)
+        a, b = t_hi[rows_of, cols], t_lo[rows_of, cols]
+        total = jnp.dot(hi, a, preferred_element_type=jnp.float32)
+        total = total + jnp.dot(hi, b, preferred_element_type=jnp.float32)
+        total = total + jnp.dot(lo, a, preferred_element_type=jnp.float32)
+        filt[at, pl.ds(first, width)] = total
+        for i in range(width // 128):
+            sums[at, :] += total[:, i * 128 : (i + 1) * 128]
 
     for k in range(CHUNKS):
         for d in range(4):
@@ -164,25 +175,38 @@
             def _():
                 halo_wait(d, k)
 
+        lanes = pl.ds(EDGES[k], EDGES[k + 1] - EDGES[k])
+        shifted = pl.ds(EDGES[k] + REACH, EDGES[k + 1] - EDGES[k])
+        first = max(0, EDGES[k] - REACH)
+        last = FRAMES if k == CHUNKS - 1 else EDGES[k + 1] - REACH
+
         def outer(h, _):
             at = pl.ds(pl.multiple_of(h * half, half), half)
-            smooth[at, 128 + k * CHUNK : 128 + (k + 1) * CHUNK] += product(halo, VOXELS, k, h)
+            s_hi[at, shifted], s_lo[at, shifted] = split(filt[at, lanes] + product(halo, VOXELS, lanes, h))
+            for start in range(first, last, FILTER):
+                filter_part(at, start, min(FILTER, last - start))
             return 0
 
         lax.fori_loop(0, 2, outer, 0)
-        first = max(0, k * CHUNK - 128)
-        last = FRAMES if k == CHUNKS - 1 else (k + 1) * CHUNK - 128
-        filter_part(first, last - first)
+
+    deep = 64
 
     def norm(t, _):
-        at = pl.ds(pl.multiple_of(t * 16, 16), 16)
-        f = filt[at, :]
-        centred = f - jnp.mean(f, axis=1, keepdims=True)
-        scale = lax.rsqrt(jnp.mean(centred * centred, axis=1, keepdims=True) + 1e-05)
-        rows[at, :] = (centred * scale).astype(jnp.bfloat16)
-        return 0
-
-    lax.fori_loop(0, PANEL // 16, norm, 0)
+        at = pl.ds(pl.multiple_of(t * deep, deep), deep)
+        mean = jnp.sum(sums[at, :], axis=1, keepdims=True) * (1.0 / FRAMES)
+        wide_mean = jnp.broadcast_to(mean, (deep, 128))
+        square = jnp.zeros((deep, 128), jnp.float32)
+        for i in range(FRAMES // 128):
+            centred = filt[at, i * 128 : (i + 1) * 128] - wide_mean
+            square = square + centred * centred
+        scale = lax.rsqrt(jnp.sum(square, axis=1, keepdims=True) * (1.0 / FRAMES) + 1e-05)
+        wide_scale = jnp.broadcast_to(scale, (deep, 128))
+        for i in range(FRAMES // 128):
+            lanes = slice(i * 128, (i + 1) * 128)
+            rows[at, lanes] = ((filt[at, lanes] - wide_mean) * wide_scale).astype(jnp.bfloat16)
+        return 0
+
+    lax.fori_loop(0, PANEL // deep, norm, 0)
 
     for k in range(CHUNKS):
         for d in range(4):
@@ -205,8 +229,12 @@
             pltpu.VMEM((PANEL, 128), jnp.int32),
             pltpu.VMEM((PANEL, 2 * VOXELS), jnp.bfloat16),
             pltpu.VMEM((PANEL, 2 * VOXELS), jnp.bfloat16),
-            pltpu.VMEM((PANEL, FRAMES + 256), jnp.float32),
+            pltpu.VMEM((PANEL, FRAMES + 2 * REACH), jnp.bfloat16),
+            pltpu.VMEM((PANEL, FRAMES + 2 * REACH), jnp.bfloat16),
+            pltpu.VMEM((FILTER + 2 * REACH, FILTER), jnp.bfloat16),
+            pltpu.VMEM((FILTER + 2 * REACH, FILTER), jnp.bfloat16),
             pltpu.VMEM((PANEL, FRAMES), jnp.float32),
+            pltpu.VMEM((PANEL, 128), jnp.float32),
             pltpu.SemaphoreType.DMA,
             pltpu.SemaphoreType.DMA((4, CHUNKS)),
             pltpu.SemaphoreType.DMA((4, CHUNKS)),
@@ -218,7 +246,7 @@
     )(signal, chosen, wclass, kernel, taps)
 
 
-def group_kernel(rows, tiles, held, stage, own_sem, swap_sem, x_sem, up_sem, down_sem, core_sem, recv_sem, out_sem):
+def group_kernel(rows, tiles, held, near_out, near_in, last_out, last_in, swap_sem, x_sem, up_sem, down_sem, core_sem, recv_sem, lend_sem, borrow_sem):
     loop, slab = lax.axis_index("loop"), lax.axis_index("slab")
     x, z, c = loop // 8, (loop // 2) % 4, loop % 2
     y, h = slab // 2, slab % 2
@@ -271,6 +299,10 @@
         swaps[i].start()
 
     mine, other = panel(x, z), panel(1 - x, z)
+    y_last = (y + 2) % 4
+    for pz in (z_down, z_up, z_far):
+        for pc in range(2):
+            held[panel(x, pz, pc), y_last, 1 - h] = jnp.zeros((SHARE, FRAMES), jnp.bfloat16)
 
     def begin(p, _):
         py = at(p)
@@ -299,19 +331,19 @@
         py = at(p)
         even = p % 2 == 0
         for pz, sem, peer, on in ((z_down, up_sem, up, even), (z_up, down_sem, down, jnp.logical_not(even))):
-            for px, ph in ((x, h), (1 - x, 1 - h)):
-                q = panel(px, pz)
+            for q, ph in ((panel(x, pz), h), (panel(1 - x, pz), 1 - h)):
                 arrived(q, py, ph)
 
                 @pl.when(on)
                 def _():
                     copy(q, py, ph, sem, peer).start()
-                if px is x:
-                    copy(q, py, ph, x_sem, across).start()
                 copy(q, py, ph, core_sem, sibling).start()
         arrived(mine, py, 1 - h)
-        copy(mine, py, 1 - h, up_sem, up).start()
-        copy(mine, py, 1 - h, down_sem, down).start()
+
+        @pl.when(p < 3)
+        def _():
+            copy(mine, py, 1 - h, up_sem, up).start()
+            copy(mine, py, 1 - h, down_sem, down).start()
         copy(mine, py, 1 - h, core_sem, sibling).start()
         arrived(other, py, h)
         copy(other, py, h, core_sem, sibling).start()
@@ -319,160 +351,211 @@
 
     lax.fori_loop(0, 4, second, 0)
 
-    def from_sibling(px, pz):
-        def body(i, _):
-            arrived(panel(px, pz, 1 - c), i // 2, i % 2)
+    def from_sibling(px, pz, ph, count=4):
+        def body(p, _):
+            arrived(panel(px, pz, 1 - c), at(p), ph)
             return 0
 
-        lax.fori_loop(0, 8, body, 0)
-
-    def tile(q):
-        left = held[loop].reshape(PANEL, FRAMES)
+        lax.fori_loop(0, count, body, 0)
+
+    def times(q, right):
+        left = held[q].reshape(PANEL, FRAMES)
+        product = lax.dot_general(left, right, (((1,), (1,)), ((), ())), preferred_element_type=jnp.float32)
+        return product * (1.0 / FRAMES**0.5)
+
+    def lend(j, i):
+        if i < 2:
+            src, dst = near_out.at[j, i], near_in.at[j, i]
+        else:
+            src, dst = last_out.at[j], last_in.at[j]
+        return pltpu.make_async_remote_copy(
+            src_ref=src, dst_ref=dst, send_sem=lend_sem.at[j, i], recv_sem=borrow_sem.at[j, i], device_id=across, device_id_type=MESH
+        )
+
+    def compute_for_across(j, pz):
+        from_sibling(x, pz, h)
+        from_sibling(1 - x, pz, 1 - h)
+        for pc in range(2):
+            right = held[panel(x, pz, pc), :, h].reshape(PANEL // 2, FRAMES)
+            near_out[j, pc] = times(other, right).astype(jnp.bfloat16)
+            lend(j, pc).start()
+        right = jnp.concatenate([held[panel(1 - x, pz, pc), y_last, 1 - h] for pc in range(2)], axis=0)
+        last_out[j] = times(other, right).astype(jnp.bfloat16)
+        lend(j, 2).start()
+
+    def columns(q, first, width):
+        return pl.ds(pl.multiple_of(q * PANEL + first, 128), width)
+
+    def full(q):
         for j in range(2):
             right = held[q, 2 * j : 2 * j + 2].reshape(PANEL // 2, FRAMES)
-            product = lax.dot_general(left, right, (((1,), (1,)), ((), ())), preferred_element_type=jnp.float32)
-            stage[q, :, j * 256 : (j + 1) * 256] = (product * (1.0 / FRAMES**0.5)).astype(jnp.bfloat16)
-        tile_copy(q).start()
-
-    def tile_copy(q):
-        return pltpu.make_async_copy(
-            stage.at[q], tiles.at[:, pl.ds(pl.multiple_of(q * PANEL, PANEL), PANEL)], out_sem.at[q]
-        )
-
-    def both(px, pz):
-        from_sibling(px, pz)
+            tiles[:, columns(q, j * 256, 256)] = times(loop, right).astype(jnp.bfloat16)
+
+    def whole(px):
+        from_sibling(px, z, 0)
+        from_sibling(px, z, 1)
 
         def body(pc, _):
-            tile(panel(px, pz, pc))
+            q = panel(px, z, pc)
+            full(q)
             return 0
 
         lax.fori_loop(0, 2, body, 0)
+
+    lane = lax.broadcasted_iota(jnp.int32, (PANEL, 128), 1)
+
+    def same_column(j, pz):
+        from_sibling(x, pz, 1 - h, 3)
+        lend(j, 2).wait_recv()
+
+        def body(pc, _):
+            q = panel(x, pz, pc)
+            full(q)
+            part = last_in[j].astype(jnp.float32)
+            part = jnp.where(pc == 1 - h, part, pltpu.roll(part, 64, axis=1))
+            place = columns(q, y_last * 128, 128)
+            keep = tiles[:, place].astype(jnp.float32)
+            tiles[:, place] = jnp.where(lane // 64 == 1 - h, part, keep).astype(jnp.bfloat16)
+            return 0
+
+        lax.fori_loop(0, 2, body, 0)
+
+    def other_column(j, pz):
+        for pc in range(2):
+            lend(j, pc).wait_recv()
+
+        def body(pc, _):
+            q = panel(1 - x, pz, pc)
+            here = times(loop, held[q, :, 1 - h].reshape(PANEL // 2, FRAMES))
+            there = near_in[j, pc].astype(jnp.float32)
+            low, high = jnp.where(h == 0, there, here), jnp.where(h == 0, here, there)
+            for i in range(2):
+                a, b = low[:, i * 128 : (i + 1) * 128], high[:, i * 128 : (i + 1) * 128]
+                first = jnp.where(lane < 64, a, pltpu.roll(b, 64, axis=1))
+                after = jnp.where(lane < 64, pltpu.roll(a, 64, axis=1), b)
+                tiles[:, columns(q, i * 256, 128)] = first.astype(jnp.bfloat16)
+                tiles[:, columns(q, i * 256 + 128, 128)] = after.astype(jnp.bfloat16)
+            return 0
+
+        lax.fori_loop(0, 2, body, 0)
+
+    def beside(body):
+        def step(j, _):
+            body(j, jnp.where(j == 0, z_down, z_up))
+            return 0
+
+        lax.fori_loop(0, 2, step, 0)
+
+    beside(compute_for_across)
 
     def third(p, _):
         py = at(p)
-        q = panel(x, z_far)
-        arrived(q, py, h)
-        copy(q, py, h, x_sem, across).start()
-        copy(q, py, h, core_sem, sibling).start()
         even = p % 2 == 0
-        for pz, sem, peer, on in ((z_down, up_sem, up, even), (z_up, down_sem, down, jnp.logical_not(even))):
-            q = panel(x, pz)
-            arrived(q, py, 1 - h)
-
-            @pl.when(on)
-            def _():
-                copy(q, py, 1 - h, sem, peer).start()
-            copy(q, py, 1 - h, core_sem, sibling).start()
-        q = panel(1 - x, z_far)
-        arrived(q, py, 1 - h)
-        copy(q, py, 1 - h, core_sem, sibling).start()
+        for q, ph in ((panel(x, z_far), h), (panel(1 - x, z_far), 1 - h)):
+            arrived(q, py, ph)
+            copy(q, py, ph, core_sem, sibling).start()
+
+        @pl.when(p < 3)
+        def _():
+            for pz, sem, peer, on in ((z_down, up_sem, up, even), (z_up, down_sem, down, jnp.logical_not(even))):
+                q = panel(x, pz)
+                arrived(q, py, 1 - h)
+
+                @pl.when(on)
+                def _():
+                    copy(q, py, 1 - h, sem, peer).start()
+                copy(q, py, 1 - h, core_sem, sibling).start()
         return 0
 
     lax.fori_loop(0, 4, third, 0)
+    compute_for_across(2, z_far)
 
     def near(i, _):
-        both(jnp.where(i == 0, x, 1 - x), z)
+        whole(jnp.where(i == 0, x, 1 - x))
         return 0
 
     lax.fori_loop(0, 2, near, 0)
+    beside(other_column)
 
     def fourth(p, _):
-        py = at(p)
-        for pz in (z_down, z_up):
-            q = panel(1 - x, pz)
-            arrived(q, py, h)
-            copy(q, py, h, core_sem, sibling).start()
-        return 0
-
-    lax.fori_loop(0, 4, fourth, 0)
-
-    def beside(i, _):
-        both(x, jnp.where(i == 0, z_down, z_up))
-        return 0
-
-    lax.fori_loop(0, 2, beside, 0)
-
-    def fifth(p, _):
         py = at(p)
         q = panel(x, z_far)
         arrived(q, py, 1 - h)
         copy(q, py, 1 - h, core_sem, sibling).start()
         return 0
 
-    lax.fori_loop(0, 4, fifth, 0)
-
-    def beyond(i, _):
-        both(jnp.where(i == 2, x, 1 - x), jnp.where(i == 0, z_down, jnp.where(i == 1, z_up, z_far)))
-        return 0
-
-    lax.fori_loop(0, 3, beyond, 0)
-
-    def sixth(p, _):
-        py = at(p)
-        q = panel(1 - x, z_far)
-        arrived(q, py, h)
-        copy(q, py, h, core_sem, sibling).start()
-        return 0
-
-    lax.fori_loop(0, 4, sixth, 0)
-    both(1 - x, z_far)
+    lax.fori_loop(0, 3, fourth, 0)
+    beside(same_column)
+    other_column(2, z_far)
+    same_column(2, z_far)
 
     for swap in swaps:
         swap.wait_send()
+
+    for j in range(3):
+        for i in range(3):
+            lend(j, i).wait_send()
 
     def left(p, _):
         py = at(p)
         even = p % 2 == 0
-        for pz in range(4):
-            q = panel(x, pz)
-            copy(q, py, h, x_sem, across).wait_send()
-            for px in range(2):
-                for ph in range(2):
-                    copy(panel(px, pz), py, ph, core_sem, sibling).wait_send()
+        odd = jnp.logical_not(even)
+        copy(mine, py, h, x_sem, across).wait_send()
         copy(other, py, 1 - h, x_sem, across).wait_send()
-        for q, ph in ((mine, h), (other, 1 - h), (mine, 1 - h)):
+        for q, ph in ((mine, h), (other, 1 - h)):
             copy(q, py, ph, up_sem, up).wait_send()
             copy(q, py, ph, down_sem, down).wait_send()
-        for px, ph in ((x, h), (1 - x, 1 - h), (x, 1 - h)):
-            @pl.when(even)
+        for ph in range(2):
+            copy(mine, py, ph, core_sem, sibling).wait_send()
+            copy(other, py, ph, core_sem, sibling).wait_send()
+        for pz in (z_down, z_up, z_far):
+            copy(panel(x, pz), py, h, core_sem, sibling).wait_send()
+            copy(panel(1 - x, pz), py, 1 - h, core_sem, sibling).wait_send()
+
+        @pl.when(p < 3)
+        def _():
+            copy(mine, py, 1 - h, up_sem, up).wait_send()
+            copy(mine, py, 1 - h, down_sem, down).wait_send()
+            for pz in (z_down, z_up, z_far):
+                copy(panel(x, pz), py, 1 - h, core_sem, sibling).wait_send()
+
+        for px, ph, on in ((x, h, True), (1 - x, 1 - h, True), (x, 1 - h, p < 3)):
+            @pl.when(jnp.logical_and(even, on))
             def _():
                 copy(panel(px, z_down), py, ph, up_sem, up).wait_send()
 
-            @pl.when(jnp.logical_not(even))
+            @pl.when(jnp.logical_and(odd, on))
             def _():
                 copy(panel(px, z_up), py, ph, down_sem, down).wait_send()
         return 0
 
     lax.fori_loop(0, 4, left, 0)
-
-    def written(q, _):
-        tile_copy(q).wait()
-        return 0
-
-    lax.fori_loop(0, N_LOOP, written, 0)
 
 
 def group(rows):
     block = (N_LOOP, 4, 2)
     return pl.pallas_call(
         group_kernel,
-        out_shape=jax.ShapeDtypeStruct((PANEL, N_LOOP * PANEL), jnp.bfloat16),
+        out_shape=pltpu.VMEM((PANEL, N_LOOP * PANEL), jnp.bfloat16),
         in_specs=[pl.BlockSpec(memory_space=pltpu.VMEM)],
-        out_specs=pl.BlockSpec(memory_space=pl.ANY),
+        out_specs=pl.BlockSpec(memory_space=pltpu.VMEM),
         scratch_shapes=[
             pltpu.VMEM(block + (SHARE, FRAMES), jnp.bfloat16),
-            pltpu.VMEM((N_LOOP, PANEL, PANEL), jnp.bfloat16),
-            pltpu.SemaphoreType.DMA,
+            pltpu.VMEM((3, 2, PANEL, PANEL // 2), jnp.bfloat16),
+            pltpu.VMEM((3, 2, PANEL, PANEL // 2), jnp.bfloat16),
+            pltpu.VMEM((3, PANEL, 128), jnp.bfloat16),
+            pltpu.VMEM((3, PANEL, 128), jnp.bfloat16),
             pltpu.SemaphoreType.DMA((7,)),
             pltpu.SemaphoreType.DMA(block),
             pltpu.SemaphoreType.DMA(block),
             pltpu.SemaphoreType.DMA(block),
             pltpu.SemaphoreType.DMA(block),
             pltpu.SemaphoreType.DMA(block),
-            pltpu.SemaphoreType.DMA((N_LOOP,)),
+            pltpu.SemaphoreType.DMA((3, 3)),
+            pltpu.SemaphoreType.DMA((3, 3)),
         ],
         compiler_params=pltpu.CompilerParams(
-            collective_id=1, has_side_effects=True, vmem_limit_bytes=56 * 2**20
+            collective_id=1, has_side_effects=True, vmem_limit_bytes=46 * 2**20
         ),
         name="group",
     )(rows)

time: 211 us -> 194 us (0.919)
  Pallas kernels: 203 us -> 191 us
  local copies, waits for them, and re-layouts: 7.77 us -> 3.4 us
    pallas_call x1, Pallas kernels: 60.3 us -> 53.6 us  [front(): pl.pallas_call(front_kernel, out_shape=jax.ShapeDtypeStruct((PANEL, FRAME...]
    pallas_call x1, Pallas kernels: 142 us -> 137 us  [group(): pl.pallas_call(group_kernel, out_shape=pltpu.VMEM((PANEL, N_LOOP * PANEL)...]
    unnamed x1, local copies, waits for them, and re-layouts: 7.77 us -> 3.4 us
where the time goes in v2:
time: 194 us
  Pallas kernels  191 us (98%)
  local copies, waits for them, and re-layouts  3.4 us (2%)
    pallas_call x1, Pallas kernels, group(): pl.pallas_call(group_kernel, out_shape=pltpu.VMEM((PANEL, N_LOOP * PANEL)...  137 us
    pallas_call x1, Pallas kernels, front(): pl.pallas_call(front_kernel, out_shape=jax.ShapeDtypeStruct((PANEL, FRAME...  53.6 us

profile of v2, /device:TPU:1, one launch (start us, length us, event | category | flops | bytes accessed | tf_op | source)
XLA Modules:
  0.0 193.9 jit_solution(5604621439909571759)
XLA Ops:
  0.0 53.6 %front.1 = bf16[512,1920]{1,0:T(8,128)(2,1)} custom-call(bf16[4,4,64,1920]{3,2,1,0:T(8,128)(2,1)} %sig.1, s32[1,512]{1,0:T(1,128)} %bitcast.7, s32[16,64]{1,0:T(8,128)} %bitcast.6, f32[3,4]{1,0:T(4,128)} %kernel.1, f32[9]{0:T(128)} %taps.1), custom_call_target="tpu_custom_call" | custom-call | tf_op jit(solution)/shard_map/front/pallas_call | solution.py:221
  53.6 137.0 %group.1 = bf16[512,8192]{1,0:T(8,128)(2,1)S(1)} custom-call(bf16[4,2,64,1920]{3,2,1,0:T(8,128)(2,1)} %bitcast.5), custom_call_target="tpu_custom_call" | custom-call | tf_op jit(solution)/shard_map/group/pallas_call | solution.py:537
  190.5 3.4 %copy.7 = bf16[512,1,8192]{2,0,1:T(8,128)(2,1)} copy(bf16[512,1,8192]{2,0,1:T(8,128)(2,1)S(1)} %bitcast.4) | data formatting | bytes 16777216

commit v3 on v2

--- a/solution.py
+++ b/solution.py
@@ -21,9 +21,12 @@
 ORDER = (0, 1, 3, 2)
 
 
-def front_kernel(sig, chosen, wclass, kernel, taps, rows, block, halo, vox, w_hi, w_lo, s_hi, s_lo, t_hi, t_lo, filt, sums, load_sem, send_sem, recv_sem):
+def front_kernel(sig, chosen, wclass, kernel, taps, rows, block, halo, vox, w_hi, w_lo, s_hi, s_lo, t_hi, t_lo, filt, sums, hop, load_sem, send_sem, recv_sem, first_sem, pass_sem, hop_sem, last_sem):
     loop, slab = lax.axis_index("loop"), lax.axis_index("slab")
-    has = (slab > 0, slab < N_SLAB - 1, loop > 0, loop < N_LOOP - 1)
+    x, z, c = loop // 8, (loop // 2) % 4, loop % 2
+    is_a, is_b = loop == 7, loop == 8
+    has = (slab > 0, slab < N_SLAB - 1, jnp.logical_and(loop > 0, loop != 8), jnp.logical_and(loop < N_LOOP - 1, loop != 7))
+    edge = (slab == 0, slab == N_SLAB - 1, loop == 0, loop == N_LOOP - 1)
     peers = ((loop, slab - 1), (loop, slab + 1), (loop - 1, slab), (loop + 1, slab))
     planes = (sig.at[0], sig.at[CX - 1], sig.at[:, 0], sig.at[:, CY - 1])
     lands = (1, 0, 3, 2)
@@ -33,9 +36,53 @@
         @pl.when(there)
         def _():
             pl.semaphore_signal(barrier, inc=1, device_id=peer, device_id_type=MESH)
+    across = ((loop + 8) % N_LOOP, slab)
+    pl.semaphore_signal(barrier, inc=1, device_id=across, device_id_type=MESH)
+    for at_end, end in ((is_a, 7), (is_b, 8)):
+        low = 0 if end == 7 else 9
+
+        @pl.when(at_end)
+        def _():
+            for there in range(low, low + 7):
+                pl.semaphore_signal(barrier, inc=1, device_id=(there, slab), device_id_type=MESH)
+
+        @pl.when(jnp.logical_and(loop >= low, loop < low + 7))
+        def _():
+            pl.semaphore_signal(barrier, inc=1, device_id=(end, slab), device_id_type=MESH)
     load = pltpu.make_async_copy(sig, block, load_sem)
     load.start()
-    pl.semaphore_wait(barrier, sum(there.astype(jnp.int32) for there in has))
+    ends = jnp.where(jnp.logical_or(is_a, is_b), 7, 1)
+    pl.semaphore_wait(barrier, sum(there.astype(jnp.int32) for there in has) + 1 + ends)
+
+    def leg(src, dst, send, recv, peer):
+        return pltpu.make_async_remote_copy(
+            src_ref=src, dst_ref=dst, send_sem=send, recv_sem=recv, device_id=(peer, slab), device_id_type=MESH
+        )
+
+    def first_legs():
+        return (
+            [leg(sig.at[j, CY - 1], hop, first_sem.at[j], hop_sem, 2 * j + 1 if j < 3 else 15) for j in range(4)],
+            [leg(sig.at[j, 0], hop, first_sem.at[j], hop_sem, 8 + 2 * j if j > 0 else 0) for j in range(4)],
+        )
+
+    for at_end, legs in zip((is_a, is_b), first_legs()):
+        @pl.when(at_end)
+        def _():
+            for one in legs:
+                one.start()
+
+    early_relay = jnp.logical_and(x + c == 1, jnp.logical_not(jnp.logical_or(is_a, is_b)))
+    to_a = jnp.logical_and(x == 0, c == 0)
+    to_b = jnp.logical_and(x == 1, c == 1)
+
+    def hop_across():
+        return leg(hop, hop, pass_sem, hop_sem, across[0])
+
+    def hop_b():
+        return leg(hop, halo.at[2, z], pass_sem, last_sem.at[z], 8)
+
+    def hop_a():
+        return leg(hop, halo.at[3, z], pass_sem, last_sem.at[z], 7)
 
     def halo_copy(d, k):
         lanes = pl.ds(EDGES[k], EDGES[k + 1] - EDGES[k])
@@ -59,14 +106,17 @@
             device_id_type=MESH,
         ).wait_recv()
 
-    for k in range(CHUNKS):
-        for d in range(4):
-            @pl.when(has[d])
-            def _():
-                halo_copy(d, k).start()
+    def send_chunks(chunks):
+        for k in chunks:
+            for d in range(4):
+                @pl.when(has[d])
+                def _():
+                    halo_copy(d, k).start()
+
+    send_chunks(range(2))
 
     for d in range(4):
-        @pl.when(jnp.logical_not(has[d]))
+        @pl.when(edge[d])
         def _():
             halo[d] = jnp.zeros_like(halo[d])
     for part in (s_hi, s_lo):
@@ -134,6 +184,13 @@
 
     lax.fori_loop(0, PANEL // tall, build, 0)
 
+    @pl.when(early_relay)
+    def _():
+        hop_across().wait_recv()
+        hop_across().start()
+
+    send_chunks(range(2, CHUNKS))
+
     half = 256
 
     def product(ref, first, lanes, h):
@@ -155,6 +212,18 @@
 
     lax.fori_loop(0, FRAMES // WIDE * 2, inner, 0)
     sums[...] = jnp.zeros_like(sums)
+
+    for relay, onward in ((to_a, hop_a), (to_b, hop_b)):
+        @pl.when(relay)
+        def _():
+            hop_across().wait_recv()
+            onward().start()
+
+    for at_end, onward in ((is_a, 3), (is_b, 2)):
+        @pl.when(at_end)
+        def _():
+            for j in range(4):
+                leg(hop, halo.at[onward, j], pass_sem, last_sem.at[j], 7).wait_recv()
 
     def filter_part(at, first, width):
         window = pl.ds(first, width + 2 * REACH)
@@ -208,6 +277,16 @@
 
     lax.fori_loop(0, PANEL // deep, norm, 0)
 
+    for at_end, legs in zip((is_a, is_b), first_legs()):
+        @pl.when(at_end)
+        def _():
+            for one in legs:
+                one.wait_send()
+
+    @pl.when(jnp.logical_not(jnp.logical_or(is_a, is_b)))
+    def _():
+        hop_across().wait_send()
+
     for k in range(CHUNKS):
         for d in range(4):
             @pl.when(has[d])
@@ -220,7 +299,7 @@
     smem = pl.BlockSpec(memory_space=pltpu.SMEM)
     return pl.pallas_call(
         front_kernel,
-        out_shape=jax.ShapeDtypeStruct((PANEL, FRAMES), jnp.bfloat16),
+        out_shape=pltpu.VMEM((PANEL, FRAMES), jnp.bfloat16),
         in_specs=[pl.BlockSpec(memory_space=pl.ANY), vmem, vmem, smem, smem],
         out_specs=vmem,
         scratch_shapes=[
@@ -235,9 +314,14 @@
             pltpu.VMEM((FILTER + 2 * REACH, FILTER), jnp.bfloat16),
             pltpu.VMEM((PANEL, FRAMES), jnp.float32),
             pltpu.VMEM((PANEL, 128), jnp.float32),
+            pltpu.VMEM((CZ, FRAMES), jnp.bfloat16),
             pltpu.SemaphoreType.DMA,
             pltpu.SemaphoreType.DMA((4, CHUNKS)),
             pltpu.SemaphoreType.DMA((4, CHUNKS)),
+            pltpu.SemaphoreType.DMA((4,)),
+            pltpu.SemaphoreType.DMA,
+            pltpu.SemaphoreType.DMA,
+            pltpu.SemaphoreType.DMA((4,)),
         ],
         compiler_params=pltpu.CompilerParams(
             collective_id=0, has_side_effects=True, vmem_limit_bytes=56 * 2**20
@@ -246,22 +330,22 @@
     )(signal, chosen, wclass, kernel, taps)
 
 
-def group_kernel(rows, tiles, held, near_out, near_in, last_out, last_in, swap_sem, x_sem, up_sem, down_sem, core_sem, recv_sem, lend_sem, borrow_sem):
+def group_kernel(rows, tiles, held, x_out, x_in, z_out, z_in, swap_sem, x_sem, mate_sem, mirror_sem, core_sem, recv_sem, lend_sem, borrow_sem):
     loop, slab = lax.axis_index("loop"), lax.axis_index("slab")
     x, z, c = loop // 8, (loop // 2) % 4, loop % 2
     y, h = slab // 2, slab % 2
-    z_up, z_down, z_far = (z + 1) % 4, (z + 3) % 4, (z + 2) % 4
+    z_mate, z_mirror, z_far = z + 1 - 2 * (z % 2), 3 - z, (z + 2) % 4
 
     def panel(px, pz, pc=None):
         return px * 8 + pz * 2 + (c if pc is None else pc)
 
-    up, down = (panel(x, z_up), slab), (panel(x, z_down), slab)
+    mate, mirror = (panel(x, z_mate), slab), (panel(x, z_mirror), slab)
     across, sibling = (panel(1 - x, z), slab), (panel(x, z, 1 - c), slab)
     inside = [(loop, ((y + dy) % 4) * 2 + h) for dy in (1, 3, 2)]
     outside = [(panel(1 - x, z), ((y + dy) % 4) * 2 + 1 - h) for dy in ORDER]
 
     barrier = pltpu.get_barrier_semaphore()
-    peers = [up, down, across, sibling] + inside + outside
+    peers = [mate, mirror, across, sibling] + inside + outside
     for peer in peers:
         pl.semaphore_signal(barrier, inc=1, device_id=peer, device_id_type=MESH)
     pl.semaphore_wait(barrier, len(peers))
@@ -299,10 +383,6 @@
         swaps[i].start()
 
     mine, other = panel(x, z), panel(1 - x, z)
-    y_last = (y + 2) % 4
-    for pz in (z_down, z_up, z_far):
-        for pc in range(2):
-            held[panel(x, pz, pc), y_last, 1 - h] = jnp.zeros((SHARE, FRAMES), jnp.bfloat16)
 
     def begin(p, _):
         py = at(p)
@@ -314,219 +394,217 @@
         @pl.when(p > 0)
         def _():
             arrived(mine, py, h)
-        copy(mine, py, h, up_sem, up).start()
-        copy(mine, py, h, down_sem, down).start()
+        copy(mine, py, h, mate_sem, mate).start()
+        copy(mine, py, h, mirror_sem, mirror).start()
         copy(mine, py, h, x_sem, across).start()
         copy(mine, py, h, core_sem, sibling).start()
         arrived(other, py, 1 - h)
         copy(other, py, 1 - h, x_sem, across).start()
-        copy(other, py, 1 - h, up_sem, up).start()
-        copy(other, py, 1 - h, down_sem, down).start()
+        copy(other, py, 1 - h, mate_sem, mate).start()
         copy(other, py, 1 - h, core_sem, sibling).start()
         return 0
 
     lax.fori_loop(0, 4, begin, 0)
+
+    def onward(p, q, ph, odd):
+        @pl.when(p % 2 == odd)
+        def _():
+            if odd:
+                copy(q, at(p), ph, mate_sem, mate).start()
+            else:
+                copy(q, at(p), ph, mirror_sem, mirror).start()
 
     def second(p, _):
         py = at(p)
-        even = p % 2 == 0
-        for pz, sem, peer, on in ((z_down, up_sem, up, even), (z_up, down_sem, down, jnp.logical_not(even))):
-            for q, ph in ((panel(x, pz), h), (panel(1 - x, pz), 1 - h)):
-                arrived(q, py, ph)
-
-                @pl.when(on)
-                def _():
-                    copy(q, py, ph, sem, peer).start()
-                copy(q, py, ph, core_sem, sibling).start()
         arrived(mine, py, 1 - h)
-
-        @pl.when(p < 3)
-        def _():
-            copy(mine, py, 1 - h, up_sem, up).start()
-            copy(mine, py, 1 - h, down_sem, down).start()
+        copy(mine, py, 1 - h, mirror_sem, mirror).start()
+        copy(mine, py, 1 - h, mate_sem, mate).start()
         copy(mine, py, 1 - h, core_sem, sibling).start()
-        arrived(other, py, h)
-        copy(other, py, h, core_sem, sibling).start()
+        for pz, odd in ((z_mirror, 1), (z_mate, 0)):
+            q = panel(x, pz)
+            arrived(q, py, h)
+            onward(p, q, h, odd)
+            copy(q, py, h, core_sem, sibling).start()
+        for q, ph in ((panel(1 - x, z_mate), 1 - h), (other, h)):
+            arrived(q, py, ph)
+            copy(q, py, ph, core_sem, sibling).start()
         return 0
 
     lax.fori_loop(0, 4, second, 0)
 
-    def from_sibling(px, pz, ph, count=4):
+    def from_sibling(px, pz, ph):
         def body(p, _):
             arrived(panel(px, pz, 1 - c), at(p), ph)
             return 0
 
-        lax.fori_loop(0, count, body, 0)
+        lax.fori_loop(0, 4, body, 0)
 
     def times(q, right):
         left = held[q].reshape(PANEL, FRAMES)
         product = lax.dot_general(left, right, (((1,), (1,)), ((), ())), preferred_element_type=jnp.float32)
         return product * (1.0 / FRAMES**0.5)
 
-    def lend(j, i):
-        if i < 2:
-            src, dst = near_out.at[j, i], near_in.at[j, i]
-        else:
-            src, dst = last_out.at[j], last_in.at[j]
+    def half(q, ph):
+        return held[q, :, ph].reshape(PANEL // 2, FRAMES)
+
+    def lend(axis, j, pc):
+        out, into, peer = ((x_out, x_in, across), (z_out, z_in, mirror))[axis]
         return pltpu.make_async_remote_copy(
-            src_ref=src, dst_ref=dst, send_sem=lend_sem.at[j, i], recv_sem=borrow_sem.at[j, i], device_id=across, device_id_type=MESH
+            src_ref=out.at[j, pc],
+            dst_ref=into.at[j, pc],
+            send_sem=lend_sem.at[axis, j, pc],
+            recv_sem=borrow_sem.at[axis, j, pc],
+            device_id=peer,
+            device_id_type=MESH,
         )
 
-    def compute_for_across(j, pz):
+    def lend_across(j, pz):
         from_sibling(x, pz, h)
+
+        def body(pc, _):
+            x_out[j, pc] = times(other, half(panel(x, pz, pc), h)).astype(jnp.bfloat16)
+            lend(0, j, pc).start()
+            return 0
+
+        lax.fori_loop(0, 2, body, 0)
+
+    def lend_mirror(j, pz):
         from_sibling(1 - x, pz, 1 - h)
-        for pc in range(2):
-            right = held[panel(x, pz, pc), :, h].reshape(PANEL // 2, FRAMES)
-            near_out[j, pc] = times(other, right).astype(jnp.bfloat16)
-            lend(j, pc).start()
-        right = jnp.concatenate([held[panel(1 - x, pz, pc), y_last, 1 - h] for pc in range(2)], axis=0)
-        last_out[j] = times(other, right).astype(jnp.bfloat16)
-        lend(j, 2).start()
+
+        def body(pc, _):
+            z_out[j, pc] = times(panel(x, z_mirror), half(panel(1 - x, pz, pc), 1 - h)).astype(jnp.bfloat16)
+            lend(1, j, pc).start()
+            return 0
+
+        lax.fori_loop(0, 2, body, 0)
 
     def columns(q, first, width):
         return pl.ds(pl.multiple_of(q * PANEL + first, 128), width)
 
-    def full(q):
-        for j in range(2):
-            right = held[q, 2 * j : 2 * j + 2].reshape(PANEL // 2, FRAMES)
+    def full(px, pz):
+        def body(i, _):
+            q, j = panel(px, pz, i // 2), i % 2
+            right = held[q, pl.ds(2 * j, 2)].reshape(PANEL // 2, FRAMES)
             tiles[:, columns(q, j * 256, 256)] = times(loop, right).astype(jnp.bfloat16)
-
-    def whole(px):
-        from_sibling(px, z, 0)
-        from_sibling(px, z, 1)
-
-        def body(pc, _):
-            q = panel(px, z, pc)
-            full(q)
             return 0
 
-        lax.fori_loop(0, 2, body, 0)
+        lax.fori_loop(0, 4, body, 0)
 
     lane = lax.broadcasted_iota(jnp.int32, (PANEL, 128), 1)
 
-    def same_column(j, pz):
-        from_sibling(x, pz, 1 - h, 3)
-        lend(j, 2).wait_recv()
-
-        def body(pc, _):
-            q = panel(x, pz, pc)
-            full(q)
-            part = last_in[j].astype(jnp.float32)
-            part = jnp.where(pc == 1 - h, part, pltpu.roll(part, 64, axis=1))
-            place = columns(q, y_last * 128, 128)
-            keep = tiles[:, place].astype(jnp.float32)
-            tiles[:, place] = jnp.where(lane // 64 == 1 - h, part, keep).astype(jnp.bfloat16)
+    def place(q, same, opposite):
+        low, high = jnp.where(h == 0, same, opposite), jnp.where(h == 0, opposite, same)
+        for i in range(2):
+            a, b = low[:, i * 128 : (i + 1) * 128], high[:, i * 128 : (i + 1) * 128]
+            first = jnp.where(lane < 64, a, pltpu.roll(b, 64, axis=1))
+            after = jnp.where(lane < 64, pltpu.roll(a, 64, axis=1), b)
+            tiles[:, columns(q, i * 256, 128)] = first.astype(jnp.bfloat16)
+            tiles[:, columns(q, i * 256 + 128, 128)] = after.astype(jnp.bfloat16)
+
+    def borrowed(axis, j, pc):
+        lend(axis, j, pc).wait_recv()
+        return (x_in, z_in)[axis][j, pc].astype(jnp.float32)
+
+    def each_core(body):
+        def step(pc, _):
+            body(pc)
             return 0
 
-        lax.fori_loop(0, 2, body, 0)
-
-    def other_column(j, pz):
-        for pc in range(2):
-            lend(j, pc).wait_recv()
-
-        def body(pc, _):
-            q = panel(1 - x, pz, pc)
-            here = times(loop, held[q, :, 1 - h].reshape(PANEL // 2, FRAMES))
-            there = near_in[j, pc].astype(jnp.float32)
-            low, high = jnp.where(h == 0, there, here), jnp.where(h == 0, here, there)
-            for i in range(2):
-                a, b = low[:, i * 128 : (i + 1) * 128], high[:, i * 128 : (i + 1) * 128]
-                first = jnp.where(lane < 64, a, pltpu.roll(b, 64, axis=1))
-                after = jnp.where(lane < 64, pltpu.roll(a, 64, axis=1), b)
-                tiles[:, columns(q, i * 256, 128)] = first.astype(jnp.bfloat16)
-                tiles[:, columns(q, i * 256 + 128, 128)] = after.astype(jnp.bfloat16)
-            return 0
-
-        lax.fori_loop(0, 2, body, 0)
-
-    def beside(body):
-        def step(j, _):
-            body(j, jnp.where(j == 0, z_down, z_up))
-            return 0
-
         lax.fori_loop(0, 2, step, 0)
 
-    beside(compute_for_across)
-
     def third(p, _):
-        py = at(p)
-        even = p % 2 == 0
-        for q, ph in ((panel(x, z_far), h), (panel(1 - x, z_far), 1 - h)):
-            arrived(q, py, ph)
-            copy(q, py, ph, core_sem, sibling).start()
-
-        @pl.when(p < 3)
-        def _():
-            for pz, sem, peer, on in ((z_down, up_sem, up, even), (z_up, down_sem, down, jnp.logical_not(even))):
-                q = panel(x, pz)
-                arrived(q, py, 1 - h)
-
-                @pl.when(on)
-                def _():
-                    copy(q, py, 1 - h, sem, peer).start()
-                copy(q, py, 1 - h, core_sem, sibling).start()
+        q = panel(x, z_mirror)
+        arrived(q, at(p), 1 - h)
+        onward(p, q, 1 - h, 1)
+        copy(q, at(p), 1 - h, core_sem, sibling).start()
         return 0
 
     lax.fori_loop(0, 4, third, 0)
-    compute_for_across(2, z_far)
-
-    def near(i, _):
-        whole(jnp.where(i == 0, x, 1 - x))
-        return 0
-
-    lax.fori_loop(0, 2, near, 0)
-    beside(other_column)
+
+    def early(j, _):
+        lend_mirror(j, jnp.where(j == 0, z, z_mate))
+        lend_across(j, jnp.where(j == 0, z_mirror, z_mate))
+        return 0
+
+    lax.fori_loop(0, 2, early, 0)
 
     def fourth(p, _):
         py = at(p)
+        q = panel(x, z_mate)
+        arrived(q, py, 1 - h)
+        onward(p, q, 1 - h, 0)
+        copy(q, py, 1 - h, core_sem, sibling).start()
         q = panel(x, z_far)
-        arrived(q, py, 1 - h)
-        copy(q, py, 1 - h, core_sem, sibling).start()
-        return 0
-
-    lax.fori_loop(0, 3, fourth, 0)
-    beside(same_column)
-    other_column(2, z_far)
-    same_column(2, z_far)
+        arrived(q, py, h)
+        copy(q, py, h, core_sem, sibling).start()
+        return 0
+
+    lax.fori_loop(0, 4, fourth, 0)
+    lend_across(2, z_far)
+
+    from_sibling(x, z, 0)
+    from_sibling(x, z, 1)
+    from_sibling(1 - x, z, h)
+    from_sibling(x, z_mirror, 1 - h)
+    from_sibling(x, z_mate, 1 - h)
+
+    def whole(i, _):
+        full(jnp.where(i == 1, 1 - x, x), jnp.where(i == 2, z_mirror, jnp.where(i == 3, z_mate, z)))
+        return 0
+
+    lax.fori_loop(0, 4, whole, 0)
+
+    def part_mate(pc):
+        q = panel(1 - x, z_mate, pc)
+        place(q, borrowed(0, 1, pc), times(loop, half(q, 1 - h)))
+
+    def none_mirror(pc):
+        place(panel(1 - x, z_mirror, pc), borrowed(0, 0, pc), borrowed(1, 0, pc))
+
+    def none_far(pc):
+        place(panel(1 - x, z_far, pc), borrowed(0, 2, pc), borrowed(1, 1, pc))
+
+    each_core(part_mate)
+    each_core(none_mirror)
+
+    def fifth(p, _):
+        q = panel(x, z_far)
+        arrived(q, at(p), 1 - h)
+        copy(q, at(p), 1 - h, core_sem, sibling).start()
+        return 0
+
+    lax.fori_loop(0, 4, fifth, 0)
+    each_core(none_far)
+    from_sibling(x, z_far, 1 - h)
+    full(x, z_far)
 
     for swap in swaps:
         swap.wait_send()
-
-    for j in range(3):
-        for i in range(3):
-            lend(j, i).wait_send()
+    for axis, count in ((0, 3), (1, 2)):
+        for j in range(count):
+            for pc in range(2):
+                lend(axis, j, pc).wait_send()
 
     def left(p, _):
         py = at(p)
-        even = p % 2 == 0
-        odd = jnp.logical_not(even)
-        copy(mine, py, h, x_sem, across).wait_send()
-        copy(other, py, 1 - h, x_sem, across).wait_send()
+        for q, ph in ((mine, h), (mine, 1 - h), (other, 1 - h)):
+            copy(q, py, ph, mate_sem, mate).wait_send()
+        for q, ph in ((mine, h), (mine, 1 - h)):
+            copy(q, py, ph, mirror_sem, mirror).wait_send()
         for q, ph in ((mine, h), (other, 1 - h)):
-            copy(q, py, ph, up_sem, up).wait_send()
-            copy(q, py, ph, down_sem, down).wait_send()
+            copy(q, py, ph, x_sem, across).wait_send()
+
         for ph in range(2):
-            copy(mine, py, ph, core_sem, sibling).wait_send()
-            copy(other, py, ph, core_sem, sibling).wait_send()
-        for pz in (z_down, z_up, z_far):
-            copy(panel(x, pz), py, h, core_sem, sibling).wait_send()
-            copy(panel(1 - x, pz), py, 1 - h, core_sem, sibling).wait_send()
-
-        @pl.when(p < 3)
-        def _():
-            copy(mine, py, 1 - h, up_sem, up).wait_send()
-            copy(mine, py, 1 - h, down_sem, down).wait_send()
-            for pz in (z_down, z_up, z_far):
-                copy(panel(x, pz), py, 1 - h, core_sem, sibling).wait_send()
-
-        for px, ph, on in ((x, h, True), (1 - x, 1 - h, True), (x, 1 - h, p < 3)):
-            @pl.when(jnp.logical_and(even, on))
+            @pl.when(p % 2 == 1)
             def _():
-                copy(panel(px, z_down), py, ph, up_sem, up).wait_send()
-
-            @pl.when(jnp.logical_and(odd, on))
+                copy(panel(x, z_mirror), py, ph, mate_sem, mate).wait_send()
+
+            @pl.when(p % 2 == 0)
             def _():
-                copy(panel(px, z_up), py, ph, down_sem, down).wait_send()
+                copy(panel(x, z_mate), py, ph, mirror_sem, mirror).wait_send()
+            for q in (mine, other, panel(x, z_mate), panel(x, z_mirror), panel(x, z_far)):
+                copy(q, py, ph, core_sem, sibling).wait_send()
+        copy(panel(1 - x, z_mate), py, 1 - h, core_sem, sibling).wait_send()
         return 0
 
     lax.fori_loop(0, 4, left, 0)
@@ -534,31 +612,22 @@
 
 def group(rows):
     block = (N_LOOP, 4, 2)
+    part = (2, PANEL, PANEL // 2)
     return pl.pallas_call(
         group_kernel,
         out_shape=pltpu.VMEM((PANEL, N_LOOP * PANEL), jnp.bfloat16),
-        in_specs=[pl.BlockSpec(memory_space=pltpu.VMEM)],
+        in_specs=[pl.BlockSpec(memory_space=pl.ANY)],
         out_specs=pl.BlockSpec(memory_space=pltpu.VMEM),
-        scratch_shapes=[
-            pltpu.VMEM(block + (SHARE, FRAMES), jnp.bfloat16),
-            pltpu.VMEM((3, 2, PANEL, PANEL // 2), jnp.bfloat16),
-            pltpu.VMEM((3, 2, PANEL, PANEL // 2), jnp.bfloat16),
-            pltpu.VMEM((3, PANEL, 128), jnp.bfloat16),
-            pltpu.VMEM((3, PANEL, 128), jnp.bfloat16),
-            pltpu.SemaphoreType.DMA((7,)),
-            pltpu.SemaphoreType.DMA(block),
-            pltpu.SemaphoreType.DMA(block),
-            pltpu.SemaphoreType.DMA(block),
-            pltpu.SemaphoreType.DMA(block),
-            pltpu.SemaphoreType.DMA(block),
-            pltpu.SemaphoreType.DMA((3, 3)),
-            pltpu.SemaphoreType.DMA((3, 3)),
-        ],
+        scratch_shapes=[pltpu.VMEM(block + (SHARE, FRAMES), jnp.bfloat16)]
+        + [pltpu.VMEM((count,) + part, jnp.bfloat16) for count in (3, 3, 2, 2)]
+        + [pltpu.SemaphoreType.DMA((7,))]
+        + [pltpu.SemaphoreType.DMA(block)] * 5
+        + [pltpu.SemaphoreType.DMA((2, 3, 2))] * 2,
         compiler_params=pltpu.CompilerParams(
-            collective_id=1, has_side_effects=True, vmem_limit_bytes=46 * 2**20
+            collective_id=1, has_side_effects=True, vmem_limit_bytes=48 * 2**20
         ),
         name="group",
-    )(rows)
+    )(pltpu.with_memory_space_constraint(rows, pltpu.VMEM))
 
 
 def local(signal, width_class, kernel, taps, chosen):

time: 194 us -> 177 us (0.912)
  Pallas kernels: 191 us -> 173 us
    pallas_call x1, Pallas kernels: 137 us -> 115 us  [group(): pl.pallas_call(group_kernel, out_shape=pltpu.VMEM((PANEL, N_LOOP * PANEL)...]
    pallas_call x1, Pallas kernels: 53.6 us -> 57.9 us  [front(): pl.pallas_call(front_kernel, out_shape=pltpu.VMEM((PANEL, FRAMES), jnp.bf...]
where the time goes in v3:
time: 177 us
  Pallas kernels  173 us (98%)
  local copies, waits for them, and re-layouts  3.4 us (2%)
    pallas_call x1, Pallas kernels, group(): pl.pallas_call(group_kernel, out_shape=pltpu.VMEM((PANEL, N_LOOP * PANEL)...  115 us
    pallas_call x1, Pallas kernels, front(): pl.pallas_call(front_kernel, out_shape=pltpu.VMEM((PANEL, FRAMES), jnp.bf...  57.9 us

profile of v3, /device:TPU:1, one launch (start us, length us, event | category | flops | bytes accessed | tf_op | source)
XLA Modules:
  0.0 176.8 jit_solution(15940873109141201754)
XLA Ops:
  0.0 57.9 %front.1 = bf16[512,1920]{1,0:T(8,128)(2,1)S(1)} custom-call(bf16[4,4,64,1920]{3,2,1,0:T(8,128)(2,1)} %sig.1, s32[1,512]{1,0:T(1,128)} %bitcast.7, s32[16,64]{1,0:T(8,128)} %bitcast.6, f32[3,4]{1,0:T(4,128)} %kernel.1, f32[9]{0:T(128)} %taps.1), custom_call_target="tpu_custom_call" | custom-call | tf_op jit(solution)/shard_map/front/pallas_call | solution.py:300
  57.9 115.5 %group.1 = bf16[512,8192]{1,0:T(8,128)(2,1)S(1)} custom-call(bf16[4,2,64,1920]{3,2,1,0:T(8,128)(2,1)S(1)} %bitcast.5), custom_call_target="tpu_custom_call" | custom-call | tf_op jit(solution)/shard_map/group/pallas_call | solution.py:616
  173.4 3.4 %copy.7 = bf16[512,1,8192]{2,0,1:T(8,128)(2,1)} copy(bf16[512,1,8192]{2,0,1:T(8,128)(2,1)S(1)} %bitcast.4) | data formatting | bytes 16777216

commit v4 on v3

--- a/solution.py
+++ b/solution.py
@@ -330,7 +330,25 @@
     )(signal, chosen, wclass, kernel, taps)
 
 
-def group_kernel(rows, tiles, held, x_out, x_in, z_out, z_in, swap_sem, x_sem, mate_sem, mirror_sem, core_sem, recv_sem, lend_sem, borrow_sem):
+def correlate(left, right):
+    product = lax.dot_general(
+        left.reshape(PANEL, FRAMES), right, (((1,), (1,)), ((), ())), preferred_element_type=jnp.float32
+    )
+    return product * (1.0 / FRAMES**0.5)
+
+
+def interleave(h, same, opposite):
+    low, high = jnp.where(h == 0, same, opposite), jnp.where(h == 0, opposite, same)
+    lane = lax.broadcasted_iota(jnp.int32, (PANEL, 128), 1)
+    parts = []
+    for i in range(2):
+        a, b = low[:, i * 128 : (i + 1) * 128], high[:, i * 128 : (i + 1) * 128]
+        parts.append(jnp.where(lane < 64, a, pltpu.roll(b, 64, axis=1)).astype(jnp.bfloat16))
+        parts.append(jnp.where(lane < 64, pltpu.roll(a, 64, axis=1), b).astype(jnp.bfloat16))
+    return parts
+
+
+def group_kernel(rows, tiles, own, far_rest, far_part, held, x_out, x_in, z_out, z_in, swap_sem, x_sem, mate_sem, mirror_sem, core_sem, recv_sem, lend_sem, borrow_sem, own_sem):
     loop, slab = lax.axis_index("loop"), lax.axis_index("slab")
     x, z, c = loop // 8, (loop // 2) % 4, loop % 2
     y, h = slab // 2, slab % 2
@@ -360,6 +378,16 @@
             dst_ref=held.at[q, py, ph],
             send_sem=sem.at[q, py, ph],
             recv_sem=recv_sem.at[q, py, ph],
+            device_id=peer,
+            device_id_type=MESH,
+        )
+
+    def copy_far(q, py, sem, peer, src):
+        return pltpu.make_async_remote_copy(
+            src_ref=src,
+            dst_ref=far_rest.at[c, py],
+            send_sem=sem.at[q, py, 1 - h],
+            recv_sem=recv_sem.at[q, py, 1 - h],
             device_id=peer,
             device_id_type=MESH,
         )
@@ -384,53 +412,82 @@
 
     mine, other = panel(x, z), panel(1 - x, z)
 
+    def own_rest(p):
+        py = at(p)
+        arrived(mine, py, 1 - h)
+        copy(mine, py, 1 - h, mirror_sem, mirror).start()
+        copy(mine, py, 1 - h, core_sem, sibling).start()
+
     def begin(p, _):
         py = at(p)
 
         @pl.when(p == 0)
         def _():
             pltpu.make_async_copy(rows.at[y, h], held.at[loop, y, h], recv_sem.at[loop, y, h]).wait()
+            copy(mine, py, h, x_sem, across).start()
 
         @pl.when(p > 0)
         def _():
             arrived(mine, py, h)
+        copy(mine, py, h, mirror_sem, mirror).start()
         copy(mine, py, h, mate_sem, mate).start()
-        copy(mine, py, h, mirror_sem, mirror).start()
-        copy(mine, py, h, x_sem, across).start()
         copy(mine, py, h, core_sem, sibling).start()
+
+        @pl.when(p >= 2)
+        def _():
+            own_rest(p - 2)
         arrived(other, py, 1 - h)
         copy(other, py, 1 - h, x_sem, across).start()
         copy(other, py, 1 - h, mate_sem, mate).start()
         copy(other, py, 1 - h, core_sem, sibling).start()
+
+        @pl.when(p == 2)
+        def _():
+            copy(mine, at(1), h, x_sem, across).start()
         return 0
 
     lax.fori_loop(0, 4, begin, 0)
-
-    def onward(p, q, ph, odd):
+    copy(mine, at(2), h, x_sem, across).start()
+    copy(mine, at(3), h, x_sem, across).start()
+
+    def onward(p, q, odd, rest):
+        sem, peer = (mate_sem, mate) if odd else (mirror_sem, mirror)
+
         @pl.when(p % 2 == odd)
         def _():
-            if odd:
-                copy(q, at(p), ph, mate_sem, mate).start()
+            if rest:
+                copy_far(q, at(p), sem, peer, held.at[q, at(p), 1 - h]).start()
             else:
-                copy(q, at(p), ph, mirror_sem, mirror).start()
+                copy(q, at(p), h, sem, peer).start()
 
     def second(p, _):
         py = at(p)
-        arrived(mine, py, 1 - h)
-        copy(mine, py, 1 - h, mirror_sem, mirror).start()
-        copy(mine, py, 1 - h, mate_sem, mate).start()
-        copy(mine, py, 1 - h, core_sem, sibling).start()
         for pz, odd in ((z_mirror, 1), (z_mate, 0)):
             q = panel(x, pz)
             arrived(q, py, h)
-            onward(p, q, h, odd)
+            onward(p, q, odd, False)
             copy(q, py, h, core_sem, sibling).start()
-        for q, ph in ((panel(1 - x, z_mate), 1 - h), (other, h)):
-            arrived(q, py, ph)
-            copy(q, py, ph, core_sem, sibling).start()
-        return 0
-
+        q = panel(1 - x, z_mate)
+        arrived(q, py, 1 - h)
+        copy(q, py, 1 - h, core_sem, sibling).start()
+        return 0
+
+    own_rest(2)
     lax.fori_loop(0, 4, second, 0)
+    own_rest(3)
+
+    def rest_to_mate(p, _):
+        copy(mine, at(p), 1 - h, mate_sem, mate).start()
+        return 0
+
+    lax.fori_loop(0, 4, rest_to_mate, 0)
+
+    def came_across(p, _):
+        arrived(other, at(p), h)
+        copy(other, at(p), h, core_sem, sibling).start()
+        return 0
+
+    lax.fori_loop(0, 4, came_across, 0)
 
     def from_sibling(px, pz, ph):
         def body(p, _):
@@ -440,9 +497,7 @@
         lax.fori_loop(0, 4, body, 0)
 
     def times(q, right):
-        left = held[q].reshape(PANEL, FRAMES)
-        product = lax.dot_general(left, right, (((1,), (1,)), ((), ())), preferred_element_type=jnp.float32)
-        return product * (1.0 / FRAMES**0.5)
+        return correlate(held[q], right)
 
     def half(q, ph):
         return held[q, :, ph].reshape(PANEL // 2, FRAMES)
@@ -490,16 +545,9 @@
 
         lax.fori_loop(0, 4, body, 0)
 
-    lane = lax.broadcasted_iota(jnp.int32, (PANEL, 128), 1)
-
     def place(q, same, opposite):
-        low, high = jnp.where(h == 0, same, opposite), jnp.where(h == 0, opposite, same)
-        for i in range(2):
-            a, b = low[:, i * 128 : (i + 1) * 128], high[:, i * 128 : (i + 1) * 128]
-            first = jnp.where(lane < 64, a, pltpu.roll(b, 64, axis=1))
-            after = jnp.where(lane < 64, pltpu.roll(a, 64, axis=1), b)
-            tiles[:, columns(q, i * 256, 128)] = first.astype(jnp.bfloat16)
-            tiles[:, columns(q, i * 256 + 128, 128)] = after.astype(jnp.bfloat16)
+        for i, part in enumerate(interleave(h, same, opposite)):
+            tiles[:, columns(q, i * 128, 128)] = part
 
     def borrowed(axis, j, pc):
         lend(axis, j, pc).wait_recv()
@@ -512,47 +560,61 @@
 
         lax.fori_loop(0, 2, step, 0)
 
+    def early_across(j, _):
+        lend_across(j, jnp.where(j == 0, z_mirror, z_mate))
+        return 0
+
+    lax.fori_loop(0, 2, early_across, 0)
+
     def third(p, _):
         q = panel(x, z_mirror)
         arrived(q, at(p), 1 - h)
-        onward(p, q, 1 - h, 1)
+        onward(p, q, 1, True)
         copy(q, at(p), 1 - h, core_sem, sibling).start()
         return 0
 
     lax.fori_loop(0, 4, third, 0)
 
-    def early(j, _):
+    def to_mirror(j, _):
         lend_mirror(j, jnp.where(j == 0, z, z_mate))
-        lend_across(j, jnp.where(j == 0, z_mirror, z_mate))
-        return 0
-
-    lax.fori_loop(0, 2, early, 0)
-
-    def fourth(p, _):
-        py = at(p)
-        q = panel(x, z_mate)
-        arrived(q, py, 1 - h)
-        onward(p, q, 1 - h, 0)
-        copy(q, py, 1 - h, core_sem, sibling).start()
-        q = panel(x, z_far)
-        arrived(q, py, h)
-        copy(q, py, h, core_sem, sibling).start()
-        return 0
-
-    lax.fori_loop(0, 4, fourth, 0)
-    lend_across(2, z_far)
-
+        return 0
+
+    lax.fori_loop(0, 2, to_mirror, 0)
+
+    keep = pltpu.make_async_copy(held.at[loop], own, own_sem)
+    keep.start()
     from_sibling(x, z, 0)
     from_sibling(x, z, 1)
+    full(x, z)
+
+    def from_far(p, _):
+        q = panel(x, z_far)
+        arrived(q, at(p), h)
+        copy(q, at(p), h, core_sem, sibling).start()
+        return 0
+
+    lax.fori_loop(0, 4, from_far, 0)
+    lend_across(2, z_far)
     from_sibling(1 - x, z, h)
+    full(1 - x, z)
+
+    def fourth(p, _):
+        q = panel(x, z_mate)
+        arrived(q, at(p), 1 - h)
+        onward(p, q, 0, True)
+        copy(q, at(p), 1 - h, core_sem, sibling).start()
+        return 0
+
+    lax.fori_loop(0, 4, fourth, 0)
+
     from_sibling(x, z_mirror, 1 - h)
     from_sibling(x, z_mate, 1 - h)
 
     def whole(i, _):
-        full(jnp.where(i == 1, 1 - x, x), jnp.where(i == 2, z_mirror, jnp.where(i == 3, z_mate, z)))
-        return 0
-
-    lax.fori_loop(0, 4, whole, 0)
+        full(x, jnp.where(i == 0, z_mirror, z_mate))
+        return 0
+
+    lax.fori_loop(0, 2, whole, 0)
 
     def part_mate(pc):
         q = panel(1 - x, z_mate, pc)
@@ -564,20 +626,25 @@
     def none_far(pc):
         place(panel(1 - x, z_far, pc), borrowed(0, 2, pc), borrowed(1, 1, pc))
 
+    def first_far(pc):
+        far_part[pc] = times(loop, half(panel(x, z_far, pc), h)).astype(jnp.bfloat16)
+
     each_core(part_mate)
+    each_core(first_far)
     each_core(none_mirror)
 
     def fifth(p, _):
         q = panel(x, z_far)
         arrived(q, at(p), 1 - h)
-        copy(q, at(p), 1 - h, core_sem, sibling).start()
+        copy_far(q, at(p), core_sem, sibling, far_rest.at[c, at(p)]).start()
         return 0
 
     lax.fori_loop(0, 4, fifth, 0)
     each_core(none_far)
+
     from_sibling(x, z_far, 1 - h)
-    full(x, z_far)
-
+
+    keep.wait()
     for swap in swaps:
         swap.wait_send()
     for axis, count in ((0, 3), (1, 2)):
@@ -602,8 +669,10 @@
             @pl.when(p % 2 == 0)
             def _():
                 copy(panel(x, z_mate), py, ph, mirror_sem, mirror).wait_send()
-            for q in (mine, other, panel(x, z_mate), panel(x, z_mirror), panel(x, z_far)):
+            for q in (mine, other, panel(x, z_mate), panel(x, z_mirror)):
                 copy(q, py, ph, core_sem, sibling).wait_send()
+        copy(panel(x, z_far), py, h, core_sem, sibling).wait_send()
+        copy_far(panel(x, z_far), py, core_sem, sibling, far_rest.at[c, py]).wait_send()
         copy(panel(1 - x, z_mate), py, 1 - h, core_sem, sibling).wait_send()
         return 0
 
@@ -615,24 +684,72 @@
     part = (2, PANEL, PANEL // 2)
     return pl.pallas_call(
         group_kernel,
-        out_shape=pltpu.VMEM((PANEL, N_LOOP * PANEL), jnp.bfloat16),
+        out_shape=(
+            pltpu.VMEM((PANEL, N_LOOP * PANEL), jnp.bfloat16),
+            pltpu.VMEM((4, 2, SHARE, FRAMES), jnp.bfloat16),
+            pltpu.VMEM((2, 4, SHARE, FRAMES), jnp.bfloat16),
+            pltpu.VMEM(part, jnp.bfloat16),
+        ),
         in_specs=[pl.BlockSpec(memory_space=pl.ANY)],
-        out_specs=pl.BlockSpec(memory_space=pltpu.VMEM),
+        out_specs=(pl.BlockSpec(memory_space=pltpu.VMEM),) * 4,
         scratch_shapes=[pltpu.VMEM(block + (SHARE, FRAMES), jnp.bfloat16)]
         + [pltpu.VMEM((count,) + part, jnp.bfloat16) for count in (3, 3, 2, 2)]
         + [pltpu.SemaphoreType.DMA((7,))]
         + [pltpu.SemaphoreType.DMA(block)] * 5
-        + [pltpu.SemaphoreType.DMA((2, 3, 2))] * 2,
+        + [pltpu.SemaphoreType.DMA((2, 3, 2))] * 2
+        + [pltpu.SemaphoreType.DMA],
         compiler_params=pltpu.CompilerParams(
-            collective_id=1, has_side_effects=True, vmem_limit_bytes=48 * 2**20
+            collective_id=1, has_side_effects=True, vmem_limit_bytes=40 * 2**20
         ),
         name="group",
     )(pltpu.with_memory_space_constraint(rows, pltpu.VMEM))
 
 
+def finish_kernel(tiles, own, far_rest, far_part, out, stage, sems):
+    loop, h = lax.axis_index("loop"), lax.axis_index("slab") % 2
+    far = loop // 8 * 4 + (loop // 2 + 2) % 4
+    wide = 2 * PANEL
+
+    def columns(pair):
+        return pl.ds(pl.multiple_of(pair * wide, wide), wide)
+
+    def ready(i):
+        pair = (far + 1 + i) % 8
+        return pltpu.make_async_copy(tiles.at[:, columns(pair)], out.at[:, columns(pair)], sems.at[i])
+
+    for i in range(7):
+        ready(i).start()
+
+    def body(pc, _):
+        right = far_rest[pc].reshape(PANEL // 2, FRAMES)
+        parts = interleave(h, far_part[pc].astype(jnp.float32), correlate(own[...], right))
+        for i, part in enumerate(parts):
+            stage[:, pl.ds(pl.multiple_of(pc * PANEL + i * 128, 128), 128)] = part
+        return 0
+
+    lax.fori_loop(0, 2, body, 0)
+    last = pltpu.make_async_copy(stage, out.at[:, columns(far)], sems.at[7])
+    last.start()
+    for i in range(7):
+        ready(i).wait()
+    last.wait()
+
+
+def finish(tiles, own, far_rest, far_part):
+    return pl.pallas_call(
+        finish_kernel,
+        out_shape=jax.ShapeDtypeStruct((PANEL, N_LOOP * PANEL), jnp.bfloat16),
+        in_specs=[pl.BlockSpec(memory_space=pl.ANY)] + [pl.BlockSpec(memory_space=pltpu.VMEM)] * 3,
+        out_specs=pl.BlockSpec(memory_space=pl.ANY),
+        scratch_shapes=[pltpu.VMEM((PANEL, 2 * PANEL), jnp.bfloat16), pltpu.SemaphoreType.DMA((8,))],
+        compiler_params=pltpu.CompilerParams(vmem_limit_bytes=12 * 2**20),
+        name="finish",
+    )(*(pltpu.with_memory_space_constraint(array, pltpu.VMEM) for array in (tiles, own, far_rest, far_part)))
+
+
 def local(signal, width_class, kernel, taps, chosen):
     rows = front(signal, chosen.reshape(1, PANEL), width_class.reshape(CX * CY, CZ), kernel, taps)
-    wide = group(rows.reshape(4, 2, SHARE, FRAMES))
+    wide = finish(*group(rows.reshape(4, 2, SHARE, FRAMES)))
     return wide.reshape(PANEL, 1, N_LOOP * PANEL)
 
 

time: 177 us -> 174 us (0.983)
  local copies, waits for them, and re-layouts: 3.4 us -> 0 us
    unnamed x1 -> x0, local copies, waits for them, and re-layouts: 3.4 us -> none
    pallas_call x1 -> x2, Pallas kernels: 115 us -> 116 us  [the longest x1 113 us: group(): pl.pallas_call(group_kernel, out_shape=(pltpu.VMEM((PANEL, N_LOOP * PANEL...]
where the time goes in v4:
time: 174 us
  Pallas kernels  174 us (100%)
    pallas_call x1, Pallas kernels, group(): pl.pallas_call(group_kernel, out_shape=(pltpu.VMEM((PANEL, N_LOOP * PANEL...  113 us
    pallas_call x1, Pallas kernels, front(): pl.pallas_call(front_kernel, out_shape=pltpu.VMEM((PANEL, FRAMES), jnp.bf...  57.9 us

profile of v4, /device:TPU:1, one launch (start us, length us, event | category | flops | bytes accessed | tf_op | source)
XLA Modules:
  0.0 173.8 jit_solution(13988980155203265410)
XLA Ops:
  0.0 57.9 %front.1 = bf16[512,1920]{1,0:T(8,128)(2,1)S(1)} custom-call(bf16[4,4,64,1920]{3,2,1,0:T(8,128)(2,1)} %sig.1, s32[1,512]{1,0:T(1,128)} %bitcast.6, s32[16,64]{1,0:T(8,128)} %bitcast.5, f32[3,4]{1,0:T(4,128)} %kernel.1, f32[9]{0:T(128)} %taps.1), custom_call_target="tpu_custom_call" | custom-call | tf_op jit(solution)/shard_map/front/pallas_call | solution.py:300
  57.9 112.5 %group.1 = (bf16[512,8192]{1,0:T(8,128)(2,1)S(1)}, bf16[4,2,64,1920]{3,2,1,0:T(8,128)(2,1)S(1)}, bf16[2,4,64,1920]{3,2,1,0:T(8,128)(2,1)S(1)}, bf16[2,512,256]{2,1,0:T(8,128)(2,1)S(1)}) custom-call(bf16[4,2,64,1920]{3,2,1,0:T(8,128)(2,1)S(1)} %bitcast.4), custom_call_target="tpu_custom_call" | custom-call | tf_op jit(solution)/shard_map/group/pallas_call | solution.py:685
  170.4 3.4 %finish.1 = bf16[512,8192]{1,0:T(8,128)(2,1)} custom-call(bf16[512,8192]{1,0:T(8,128)(2,1)S(1)} %get-tuple-element.9.tiles, bf16[4,2,64,1920]{3,2,1,0:T(8,128)(2,1)S(1)} %get-tuple-element.10.own, bf16[2,4,64,1920]{3,2,1,0:T(8,128)(2,1)S(1)} %get-tuple-element.11.far_rest, bf16[2,512,256]{2,1,0:T(8,128)(2,1)S(1)} %get-tuple-element.12.far_part), custom_call_target="tpu_custom_call" | custom-call | tf_op jit(solution)/shard_map/finish/pallas_call | solution.py:739

commit v5 on v4

--- a/solution.py
+++ b/solution.py
@@ -418,20 +418,25 @@
         copy(mine, py, 1 - h, mirror_sem, mirror).start()
         copy(mine, py, 1 - h, core_sem, sibling).start()
 
-    def begin(p, _):
+    def own_first(p):
         py = at(p)
-
-        @pl.when(p == 0)
-        def _():
-            pltpu.make_async_copy(rows.at[y, h], held.at[loop, y, h], recv_sem.at[loop, y, h]).wait()
-            copy(mine, py, h, x_sem, across).start()
-
-        @pl.when(p > 0)
-        def _():
-            arrived(mine, py, h)
         copy(mine, py, h, mirror_sem, mirror).start()
         copy(mine, py, h, mate_sem, mate).start()
         copy(mine, py, h, core_sem, sibling).start()
+
+    pltpu.make_async_copy(rows.at[y, h], held.at[loop, y, h], recv_sem.at[loop, y, h]).wait()
+    copy(mine, y, h, x_sem, across).start()
+    own_first(0)
+
+    def straight(p, _):
+        arrived(mine, at(p), h)
+        own_first(p)
+        return 0
+
+    lax.fori_loop(1, 3, straight, 0)
+
+    def begin(p, _):
+        py = at(p)
 
         @pl.when(p >= 2)
         def _():
@@ -444,6 +449,7 @@
         @pl.when(p == 2)
         def _():
             copy(mine, at(1), h, x_sem, across).start()
+            straight(3, 0)
         return 0
 
     lax.fori_loop(0, 4, begin, 0)

time: 174 us -> 168 us (0.966)
  Pallas kernels: 174 us -> 168 us
    pallas_call x1, Pallas kernels: 113 us -> 107 us  [group(): pl.pallas_call(group_kernel, out_shape=(pltpu.VMEM((PANEL, N_LOOP * PANEL...]
where the time goes in v5:
time: 168 us
  Pallas kernels  168 us (100%)
    pallas_call x1, Pallas kernels, group(): pl.pallas_call(group_kernel, out_shape=(pltpu.VMEM((PANEL, N_LOOP * PANEL...  107 us
    pallas_call x1, Pallas kernels, front(): pl.pallas_call(front_kernel, out_shape=pltpu.VMEM((PANEL, FRAMES), jnp.bf...  57.9 us
    pallas_call x1, Pallas kernels, finish(): pl.pallas_call(finish_kernel, out_shape=jax.ShapeDtypeStruct((PANEL, N_LO...  3.4 us

profile of v5, /device:TPU:1, one launch (start us, length us, event | category | flops | bytes accessed | tf_op | source)
XLA Modules:
  0.0 168.1 jit_solution(18152928738945723954)
XLA Ops:
  0.0 57.9 %front.1 = bf16[512,1920]{1,0:T(8,128)(2,1)S(1)} custom-call(bf16[4,4,64,1920]{3,2,1,0:T(8,128)(2,1)} %sig.1, s32[1,512]{1,0:T(1,128)} %bitcast.6, s32[16,64]{1,0:T(8,128)} %bitcast.5, f32[3,4]{1,0:T(4,128)} %kernel.1, f32[9]{0:T(128)} %taps.1), custom_call_target="tpu_custom_call" | custom-call | tf_op jit(solution)/shard_map/front/pallas_call | solution.py:300
  57.9 106.8 %group.1 = (bf16[512,8192]{1,0:T(8,128)(2,1)S(1)}, bf16[4,2,64,1920]{3,2,1,0:T(8,128)(2,1)S(1)}, bf16[2,4,64,1920]{3,2,1,0:T(8,128)(2,1)S(1)}, bf16[2,512,256]{2,1,0:T(8,128)(2,1)S(1)}) custom-call(bf16[4,2,64,1920]{3,2,1,0:T(8,128)(2,1)S(1)} %bitcast.4), custom_call_target="tpu_custom_call" | custom-call | tf_op jit(solution)/shard_map/group/pallas_call | solution.py:691
  164.7 3.4 %finish.1 = bf16[512,8192]{1,0:T(8,128)(2,1)} custom-call(bf16[512,8192]{1,0:T(8,128)(2,1)S(1)} %get-tuple-element.9.tiles, bf16[4,2,64,1920]{3,2,1,0:T(8,128)(2,1)S(1)} %get-tuple-element.10.own, bf16[2,4,64,1920]{3,2,1,0:T(8,128)(2,1)S(1)} %get-tuple-element.11.far_rest, bf16[2,512,256]{2,1,0:T(8,128)(2,1)S(1)} %get-tuple-element.12.far_part), custom_call_target="tpu_custom_call" | custom-call | tf_op jit(solution)/shard_map/finish/pallas_call | solution.py:745

commit v6 on v5

--- a/solution.py
+++ b/solution.py
@@ -431,6 +431,10 @@
     def straight(p, _):
         arrived(mine, at(p), h)
         own_first(p)
+
+        @pl.when(p == 1)
+        def _():
+            copy(mine, at(1), h, x_sem, across).start()
         return 0
 
     lax.fori_loop(1, 3, straight, 0)
@@ -448,12 +452,12 @@
 
         @pl.when(p == 2)
         def _():
-            copy(mine, at(1), h, x_sem, across).start()
-            straight(3, 0)
+            copy(mine, at(2), h, x_sem, across).start()
+            arrived(mine, at(3), h)
+            own_first(3)
         return 0
 
     lax.fori_loop(0, 4, begin, 0)
-    copy(mine, at(2), h, x_sem, across).start()
     copy(mine, at(3), h, x_sem, across).start()
 
     def onward(p, q, odd, rest):
@@ -473,9 +477,6 @@
             arrived(q, py, h)
             onward(p, q, odd, False)
             copy(q, py, h, core_sem, sibling).start()
-        q = panel(1 - x, z_mate)
-        arrived(q, py, 1 - h)
-        copy(q, py, 1 - h, core_sem, sibling).start()
         return 0
 
     own_rest(2)
@@ -489,6 +490,9 @@
     lax.fori_loop(0, 4, rest_to_mate, 0)
 
     def came_across(p, _):
+        q = panel(1 - x, z_mate)
+        arrived(q, at(p), 1 - h)
+        copy(q, at(p), 1 - h, core_sem, sibling).start()
         arrived(other, at(p), h)
         copy(other, at(p), h, core_sem, sibling).start()
         return 0

time: 168 us -> 168 us (level)
  no operation moved by 1% of the time
where the time goes in v6:
time: 168 us
  Pallas kernels  168 us (100%)
    pallas_call x1, Pallas kernels, group(): pl.pallas_call(group_kernel, out_shape=(pltpu.VMEM((PANEL, N_LOOP * PANEL...  107 us
    pallas_call x1, Pallas kernels, front(): pl.pallas_call(front_kernel, out_shape=pltpu.VMEM((PANEL, FRAMES), jnp.bf...  57.9 us
    pallas_call x1, Pallas kernels, finish(): pl.pallas_call(finish_kernel, out_shape=jax.ShapeDtypeStruct((PANEL, N_LO...  3.4 us

profile of v6, /device:TPU:1, one launch (start us, length us, event | category | flops | bytes accessed | tf_op | source)
XLA Modules:
  0.0 168.1 jit_solution(2585818396231864225)
XLA Ops:
  0.0 57.9 %front.1 = bf16[512,1920]{1,0:T(8,128)(2,1)S(1)} custom-call(bf16[4,4,64,1920]{3,2,1,0:T(8,128)(2,1)} %sig.1, s32[1,512]{1,0:T(1,128)} %bitcast.6, s32[16,64]{1,0:T(8,128)} %bitcast.5, f32[3,4]{1,0:T(4,128)} %kernel.1, f32[9]{0:T(128)} %taps.1), custom_call_target="tpu_custom_call" | custom-call | tf_op jit(solution)/shard_map/front/pallas_call | solution.py:300
  57.9 106.8 %group.1 = (bf16[512,8192]{1,0:T(8,128)(2,1)S(1)}, bf16[4,2,64,1920]{3,2,1,0:T(8,128)(2,1)S(1)}, bf16[2,4,64,1920]{3,2,1,0:T(8,128)(2,1)S(1)}, bf16[2,512,256]{2,1,0:T(8,128)(2,1)S(1)}) custom-call(bf16[4,2,64,1920]{3,2,1,0:T(8,128)(2,1)S(1)} %bitcast.4), custom_call_target="tpu_custom_call" | custom-call | tf_op jit(solution)/shard_map/group/pallas_call | solution.py:695
  164.7 3.4 %finish.1 = bf16[512,8192]{1,0:T(8,128)(2,1)} custom-call(bf16[512,8192]{1,0:T(8,128)(2,1)S(1)} %get-tuple-element.9.tiles, bf16[4,2,64,1920]{3,2,1,0:T(8,128)(2,1)S(1)} %get-tuple-element.10.own, bf16[2,4,64,1920]{3,2,1,0:T(8,128)(2,1)S(1)} %get-tuple-element.11.far_rest, bf16[2,512,256]{2,1,0:T(8,128)(2,1)S(1)} %get-tuple-element.12.far_part), custom_call_target="tpu_custom_call" | custom-call | tf_op jit(solution)/shard_map/finish/pallas_call | solution.py:749
